TPU v7x, 32 devices: a whole 2x2x4 slice. The times are simulated.
32 devices in a mesh: group: 2 (over y), expert: 4 (over z), tensor: 2 (over x), node: 2 (over core).
Axes of the slice: x: 2, y: 2, z: 4, core: 2. Of those that a mesh axis runs over, the one named last changes fastest.
Arguments:
- tokens: bfloat16 [1024, 7168], P(('group', 'expert'), ('tensor', 'node')), parts along dimension 0, may hold values from -6 to 6
- expert_ids: int32 [1024, 2], P(('group', 'expert')), parts along dimension 0, may hold values from 0 to 3, all different within a row; in each aligned block of 128 rows (0 to 127, 128 to 255, ...) at most 128 rows name the same one
- gate_weights: float32 [1024, 2], P(('group', 'expert')), parts along dimension 0, may hold values from 0.1 to 1
- gate_weight: bfloat16 [4, 1792, 7168], P('expert', ('tensor', 'node')), may hold values from -0.0625 to 0.0625
- up_weight: bfloat16 [4, 1792, 7168], P('expert', ('tensor', 'node')), may hold values from -0.0625 to 0.0625
- down_weight: bfloat16 [4, 1792, 7168], P('expert', None, ('tensor', 'node')), may hold values from -0.125 to 0.125
Outputs:
- mixed: bfloat16 [1024, 7168], P(('group', 'expert'), ('tensor', 'node')), parts along dimension 0
There are 2 independent parts, one for each index of `group`. A program takes and returns all parts, laid end to end along the dimension named above; an argument that names none is the same for every part. Nothing has to cross between parts.
Inputs may be any that keep to these rules, and one draw needn't show every extreme that they name: `expert_ids`: each token names 2 different experts; among the 128 tokens of one aligned block no expert is named by more than 128 tokens, and in every draw some expert is named by exactly 128 tokens of some block.
All inputs are finite; a program needn't handle non-finite values.
Results may differ from a plain program's by a relative error of at most 0.0058.
Values may be sent and summed in bfloat16 or wider, within the bound.
No kernel may reach another device: no remote copies, remote signals or barrier semaphores. Data moves between devices by JAX's collectives and lax.ppermute only.
A program may use at most 128 MiB of HBM per device.

v0:
```python
import jax
import jax.numpy as jnp
from jax import lax
from jax.sharding import PartitionSpec as P


def route_positions(expert_ids, experts):
    flat_ids = expert_ids.reshape(-1)
    count = flat_ids.shape[0]
    one_hot = (flat_ids[:, None] == jnp.arange(experts, dtype=jnp.int32)[None, :]).astype(
        jnp.float32
    )
    earlier = (
        jnp.arange(count, dtype=jnp.int32)[:, None] > jnp.arange(count, dtype=jnp.int32)[None, :]
    ).astype(jnp.float32)
    before = jnp.dot(earlier, one_hot, precision=lax.Precision.HIGHEST)
    position = jnp.sum(before * one_hot, axis=1).astype(jnp.int32)
    return (flat_ids, position)


def slot_sources(target, top_slots, slots_total, count_rows):
    source_row = jnp.arange(target.shape[0], dtype=jnp.int32) // top_slots
    match = target[None, :] == jnp.arange(slots_total, dtype=jnp.int32)[:, None]
    picked = jnp.sum(jnp.where(match, source_row[None, :], 0), axis=1)
    filled = jnp.any(match, axis=1)
    return jnp.where(filled, picked, count_rows)


def pack_rows(rows, slot_table, experts, capacity):
    padded = jnp.concatenate([rows, jnp.zeros((1, rows.shape[1]), rows.dtype)], axis=0)
    return jnp.take(padded, slot_table, axis=0).reshape(experts, capacity, rows.shape[1])


def shards(tokens, expert_ids, gate_weights, gate_weight, up_weight, down_weight):
    owners = lax.axis_size("expert")
    local_experts = gate_weight.shape[0]
    experts = local_experts * owners
    count_rows, top_slots = expert_ids.shape
    capacity = 2 * count_rows * top_slots // experts
    flat_ids, position = route_positions(expert_ids, experts)
    target = flat_ids * capacity + position
    slot_table = slot_sources(target, top_slots, experts * capacity, count_rows)
    whole = lax.all_gather(tokens, ("tensor", "node"), axis=1, tiled=True)
    packed = pack_rows(whole, slot_table, experts, capacity)
    received = lax.all_to_all(packed, "expert", split_axis=0, concat_axis=0, tiled=True)
    slots = received.shape[1]
    width = received.shape[2]
    grouped = received.reshape(owners, local_experts, slots, width)
    flat_rows = grouped[:, 0].reshape(owners * slots, width)
    contract = (((1,), (1,)), ((), ()))
    gate_part = lax.dot_general(
        flat_rows, gate_weight[0], contract, preferred_element_type=jnp.float32
    )
    up_part = lax.dot_general(flat_rows, up_weight[0], contract, preferred_element_type=jnp.float32)
    hidden = (jax.nn.silu(gate_part) * up_part).astype(jnp.bfloat16)
    block = down_weight[0]
    summed = jnp.dot(
        lax.all_gather(hidden, ("tensor", "node"), axis=1, tiled=True),
        block,
        preferred_element_type=jnp.float32,
    )
    results = [summed.astype(jnp.bfloat16).reshape(owners, slots, -1)]
    stacked = jnp.stack(results, axis=1).reshape(experts, slots, -1)
    returned = lax.all_to_all(stacked, "expert", split_axis=0, concat_axis=0, tiled=True)
    flat_out = returned.reshape(experts * capacity, -1)
    picked = jnp.take(flat_out, target, axis=0).reshape(count_rows, top_slots, -1)
    mixed = jnp.sum(picked.astype(jnp.float32) * gate_weights[:, :, None], axis=1)
    return mixed.astype(jnp.bfloat16)


def solution(mesh):
    placed = (
        P(("group", "expert"), ("tensor", "node")),
        P(("group", "expert"), None),
        P(("group", "expert"), None),
        P("expert", ("tensor", "node"), None),
        P("expert", ("tensor", "node"), None),
        P("expert", None, ("tensor", "node")),
    )
    return jax.shard_map(
        shards,
        mesh=mesh,
        in_specs=placed,
        out_specs=P(("group", "expert"), ("tensor", "node")),
        check_vma=False,
    )
```

profile of v0, /device:TPU:0, one launch (start us, length us, event | category | flops | bytes accessed | tf_op | source)
XLA Modules:
  0.0 310.8 jit_solution(10326440043833641259)
XLA Ops:
  6.5 0.7 all-gather.3.cloned.1.call-update
  7.3 0.8 copy.15
  8.1 0.1 reshape.115
  8.2 0.2 fusion.15
  8.5 0.2 fusion.16
  8.6 0.2 select_reduce_fusion
  8.8 24.0 %all-gather.3.cloned.1.call-done = bf16[128,7168]{1,0:T(8,128)(2,1)} async-done(((bf16[128,1792]{1,0:T(8,128)(2,1)}), bf16[128,7168]{1,0:T(8,128)(2,1)}) %all-gather.3.cloned.1.call-update) | async-done | bytes 1835024 | tf_op jit(solution)/shard_map/all_gather | solution.py:43
  32.8 1.7 concatenate.3
  34.5 7.1 %gather_fusion = bf16[512,7168]{1,0:T(8,128)(2,1)} fusion(bf16[129,7168]{1,0:T(8,128)(2,1)S(1)} %concatenate.3, s32[1024]{0:T(1024)S(1)} %pad_clamp_fusion.1), kind=kCustom, calls=%fused_computation | custom fusion | bytes 14682112 | tf_op jit(solution)/shard_map/jit(_take)/gather | solution.py:31
  41.5 3.8 %broadcast_select_fusion = bf16[4,128,7168]{2,1,0:T(8,128)(2,1)S(1)} fusion(bf16[4,128,7168]{2,1,0:T(8,128)(2,1)} %bitcast.31, pred[4,128]{1,0:T(4,128)(4,1)S(1)} %get-tuple-element.5), kind=kLoop, calls=%fused_computation.2 | loop fusion | flops 3670016 | bytes 14680576 | tf_op jit(solution)/shard_map/jit(_take)/select_n | solution.py:31
  45.4 165.6 %all_to_all.10 = bf16[4,128,7168]{2,1,0:T(8,128)(2,1)S(1)} all-to-all(bf16[4,128,7168]{2,1,0:T(8,128)(2,1)S(1)} %broadcast_select_fusion), channel_id=1, replica_groups=mesh['group'=2,'expert'=4,'tensor'=2,'node'=2] {'expert'}, dimensions={0} | all-to-all | bytes 14680064 | tf_op jit(solution)/shard_map/all_to_all | solution.py:45
  211.0 7.1 %fusion.4 = f32[512,448]{0,1:T(8,128)S(1)} fusion(bf16[512,7168]{1,0:T(8,128)(2,1)S(1)} %bitcast.32, bf16[1,448,7168]{2,1,0:T(8,128)(2,1)} %param.9), kind=kOutput, calls=%fused_computation.7 | convolution fusion | flops 3288334336 | bytes 14680064 | tf_op jit(solution)/shard_map/dot_general | solution.py:51
  218.2 4.3 %fusion.12 = bf16[512,448]{0,1:T(8,128)(2,1)} fusion(bf16[512,7168]{1,0:T(8,128)(2,1)S(1)} %bitcast.33, bf16[1,448,7168]{2,1,0:T(8,128)(2,1)S(1)} %bitcast.40, f32[512,448]{0,1:T(8,128)S(1)} %fusion.4), kind=kOutput, calls=%fused_computation.13 | convolution fusion | flops 3289710592 | bytes 15138816 | tf_op jit(solution)/shard_map/dot_general | solution.py:54
  222.6 19.4 %all-gather.5.cloned.1.call-done = bf16[512,1792]{0,1:T(8,128)(2,1)} async-done(((bf16[512,448]{0,1:T(8,128)(2,1)}), bf16[512,1792]{0,1:T(8,128)(2,1)}) %all-gather.5.cloned.1.call-update) | async-done | bytes 1835024 | tf_op jit(solution)/shard_map/all_gather | solution.py:58
  242.0 8.2 %fusion.6 = bf16[512,1792]{1,0:T(8,128)(2,1)} fusion(bf16[512,1792]{0,1:T(8,128)(2,1)} %all-gather.5.cloned.1.call-done, bf16[1,1792,1792]{2,1,0:T(8,128)(2,1)} %param.11), kind=kOutput, calls=%fused_computation.9 | convolution fusion | flops 3289251840 | bytes 10092544 | tf_op jit(solution)/shard_map/dot_general | solution.py:57
  250.1 4.6 %all-to-all-start.1 = ((bf16[4,128,1792]{2,1,0:T(8,128)(2,1)}), bf16[4,128,1792]{2,1,0:T(8,128)(2,1)S(1)}, u32[]{:S(2)}, u32[]{:S(2)}) async-start(bf16[4,128,1792]{2,1,0:T(8,128)(2,1)} %bitcast.34), calls=%async_computation.1 | async-start | bytes 3670016 | tf_op jit(solution)/shard_map/all_to_all | solution.py:64
  254.7 0.1 copy.18
  254.9 0.1 mul.52
  255.0 0.1 convert_element_type.38
  255.2 0.1 copy.17
  255.5 42.2 %all-to-all-done.1 = bf16[4,128,1792]{2,1,0:T(8,128)(2,1)S(1)} async-done(((bf16[4,128,1792]{2,1,0:T(8,128)(2,1)}), bf16[4,128,1792]{2,1,0:T(8,128)(2,1)S(1)}, u32[]{:S(2)}, u32[]{:S(2)}) %all-to-all-start.1) | async-done | bytes 1835040 | tf_op jit(solution)/shard_map/all_to_all | solution.py:64
  297.7 1.3 gather_fusion.1
  299.1 0.3 gather.15
  299.4 4.5 %multiply_reduce_fusion = bf16[128,1792]{1,0:T(8,128)(2,1)} fusion(bf16[128,2,1792]{2,1,0:T(2,128)(2,1)S(1)} %gather.15, pred[128,2]{1,0:T(8,128)(4,1)S(1)} %copy.17, f32[128,2]{1,0:T(8,128)S(1)} %copy.19), kind=kLoop, calls=%fused_computation.10 | loop fusion | flops 1605632 | bytes 1377536 | tf_op jit(solution)/shard_map/reduce_sum | solution.py:67
  (23 shorter events, 0.3 us)
Async XLA Ops:
  6.5 26.2 %all-gather.3.cloned.1.call-start = ((), (), s32[]{:S(2)}) async-start(), calls=%async_computation.2 | async-start | bytes 2293760 | tf_op jit(solution)/shard_map/all_gather | solution.py:43
  7.3 234.7 %all-gather.5.cloned.1.call-start = ((), (), s32[]{:S(2)}) async-start(), calls=%async_computation.3 | async-start | bytes 2293760 | tf_op jit(solution)/shard_map/all_gather | solution.py:58
  45.4 172.8 %slice-start = ((s8[6422528]{0:T(1024)(128)(4,1)}), s8[4194304]{0:T(1024)(128)(4,1)S(1)}, s32[]{:S(2)}) async-start(s8[6422528]{0:T(1024)(128)(4,1)} %bitcast.39), calls=%async_computation.4 | async-start | bytes 8388608
  211.0 7.2 %slice-start.1 = ((s8[6422528]{0:T(1024)(128)(4,1)}), s8[2228224]{0:T(1024)(128)(4,1)S(1)}, s32[]{:S(2)}) async-start(s8[6422528]{0:T(1024)(128)(4,1)} %bitcast.39), calls=%async_computation.5 | async-start | bytes 4456448
  222.5 32.2 %copy-start = (s32[128,2]{0,1:T(2,128)S(1)}, s32[128,2]{0,1:T(2,128)}, u32[]{:S(2)}) copy-start(s32[128,2]{0,1:T(2,128)} %param.7) | copy-start | bytes 3076
  222.6 32.8 %copy-start.1 = (f32[128,2]{0,1:T(2,128)S(1)}, f32[128,2]{0,1:T(2,128)}, u32[]{:S(2)}) copy-start(f32[128,2]{0,1:T(2,128)} %param.8) | copy-start | bytes 3076
  250.1 47.6 %all-to-all-start.1 = ((bf16[4,128,1792]{2,1,0:T(8,128)(2,1)}), bf16[4,128,1792]{2,1,0:T(8,128)(2,1)S(1)}, u32[]{:S(2)}, u32[]{:S(2)}) async-start(bf16[4,128,1792]{2,1,0:T(8,128)(2,1)} %bitcast.34), calls=%async_computation.1 | async-start | bytes 3670016 | tf_op jit(solution)/shard_map/all_to_all | solution.py:64
Sparse Core Ops, SparseCore 0:
  8.9 23.8 all-gather.2
  222.7 19.2 all-gather.4
where the time goes:
time: 311 us
  blocking collectives  166 us (53%)
  waiting for transfers between devices  86.3 us (28%)
  matrix products  19.8 us (6%)
  between operations  13.6 us (4%)
  local copies, waits for them, and re-layouts  12.1 us (4%)
  other arithmetic  8.74 us (3%)
  starting transfers between devices  4.64 us (1%)
    all_to_all x1, blocking collectives, shards(): lax.all_to_all(packed, 'expert', split_axis=0, concat_axis=0, tiled=True)  166 us
    all_to_all x1, waiting for transfers between devices, shards(): lax.all_to_all(stacked, 'expert', split_axis=0, concat_axis=0, tiled=True)  42.2 us
    all_gather x1, waiting for transfers between devices, shards(): whole = lax.all_gather(tokens, ('tensor', 'node'), axis=1, tiled=True)  24 us
    all_gather x1, waiting for transfers between devices, shards(): lax.all_gather(hidden, ('tensor', 'node'), axis=1, tiled=True)  19.4 us
    dot_general x1, matrix products, shards(): jnp.dot(lax.all_gather(hidden, ('tensor', 'node'), axis=1, tiled=True), b...  8.16 us
    dot_general x1, matrix products, shards(): lax.dot_general(flat_rows, gate_weight[0], contract, preferred_element_ty...  7.13 us
    gather x1, local copies, waits for them, and re-layouts, pack_rows(): jnp.take(padded, slot_table, axis=0)  7.06 us
  transfers between devices with their start and end apart: 3, of which 3 were waited for; matrix products, arithmetic and copies ran while one was open for 1% of the time, Pallas kernels for 0%

commit v1 on v0

--- a/solution.py
+++ b/solution.py
@@ -1,7 +1,13 @@
+import functools
+
 import jax
 import jax.numpy as jnp
 from jax import lax
+from jax.experimental import pallas as pl
+from jax.experimental.pallas import tpu as pltpu
 from jax.sharding import PartitionSpec as P
+
+MIB = 1 << 20
 
 
 def route_positions(expert_ids, experts):
@@ -31,7 +37,7 @@
     return jnp.take(padded, slot_table, axis=0).reshape(experts, capacity, rows.shape[1])
 
 
-def shards(tokens, expert_ids, gate_weights, gate_weight, up_weight, down_weight):
+def dispatch_shards(tokens, expert_ids, gate_weights, gate_weight, up_weight, down_weight):
     owners = lax.axis_size("expert")
     local_experts = gate_weight.shape[0]
     experts = local_experts * owners
@@ -68,6 +74,169 @@
     return mixed.astype(jnp.bfloat16)
 
 
+def gate_up_kernel(splits, order_ref, *refs):
+    pieces = refs[:4]
+    gate_ref, up_ref, out_ref, gate_acc, up_acc = refs[4:]
+    step = pl.program_id(0)
+    width = gate_ref.shape[1]
+    contract = (((1,), (1,)), ((), ()))
+
+    @pl.when(step == 0)
+    def _():
+        gate_acc[...] = jnp.zeros_like(gate_acc)
+        up_acc[...] = jnp.zeros_like(up_acc)
+
+    for j in range(4 * splits):
+
+        @pl.when(step == j)
+        def _(j=j):
+            part = j % splits
+            rows = pieces[j // splits][:, part * width : (part + 1) * width]
+            gate_acc[...] += lax.dot_general(
+                rows, gate_ref[...], contract, preferred_element_type=jnp.float32
+            )
+            up_acc[...] += lax.dot_general(
+                rows, up_ref[...], contract, preferred_element_type=jnp.float32
+            )
+
+    @pl.when(step == 4 * splits - 1)
+    def _():
+        gate = gate_acc[...]
+        out_ref[...] = (gate / (1.0 + jnp.exp(-gate)) * up_acc[...]).astype(out_ref.dtype)
+
+
+def gate_up(order, pieces, gate_weight, up_weight):
+    rows, width = pieces[0].shape
+    units = gate_weight.shape[0]
+    splits = 2
+    chunk = width // splits
+    whole = pl.BlockSpec((rows, width), lambda k, order: (0, 0))
+    weight = pl.BlockSpec(
+        (units, chunk), lambda k, order: (0, order[k // splits] * splits + k % splits)
+    )
+    return pl.pallas_call(
+        functools.partial(gate_up_kernel, splits),
+        out_shape=jax.ShapeDtypeStruct((rows, units), jnp.bfloat16),
+        grid_spec=pltpu.PrefetchScalarGridSpec(
+            num_scalar_prefetch=1,
+            grid=(4 * splits,),
+            in_specs=[whole] * 4 + [weight] * 2,
+            out_specs=pl.BlockSpec((rows, units), lambda k, order: (0, 0)),
+            scratch_shapes=[pltpu.VMEM((rows, units), jnp.float32)] * 2,
+        ),
+        compiler_params=pltpu.CompilerParams(vmem_limit_bytes=24 * MIB),
+        cost_estimate=pl.CostEstimate(
+            flops=16 * rows * width * units,
+            bytes_accessed=16 * width * units + 8 * rows * width,
+            transcendentals=rows * units,
+        ),
+        name="gate_up",
+    )(order, *pieces, gate_weight, up_weight)
+
+
+def down_kernel(order_ref, *refs):
+    pieces = refs[:4]
+    weight_ref, out_ref, acc = refs[4:]
+    step = pl.program_id(0)
+    for j in range(4):
+
+        @pl.when(step == j)
+        def _(j=j):
+            part = jnp.dot(pieces[j][...], weight_ref[...], preferred_element_type=jnp.float32)
+            if j == 0:
+                acc[...] = part
+            elif j < 3:
+                acc[...] += part
+            else:
+                out_ref[...] = (acc[...] + part).astype(out_ref.dtype)
+
+
+def down(order, pieces, weight):
+    rows, units = pieces[0].shape
+    width = weight.shape[1]
+    whole = pl.BlockSpec((rows, units), lambda k, order: (0, 0))
+    return pl.pallas_call(
+        down_kernel,
+        out_shape=jax.ShapeDtypeStruct((rows, width), jnp.bfloat16),
+        grid_spec=pltpu.PrefetchScalarGridSpec(
+            num_scalar_prefetch=1,
+            grid=(4,),
+            in_specs=[whole] * 4 + [pl.BlockSpec((units, width), lambda k, order: (order[k], 0))],
+            out_specs=pl.BlockSpec((rows, width), lambda k, order: (0, 0)),
+            scratch_shapes=[pltpu.VMEM((rows, width), jnp.float32)],
+        ),
+        compiler_params=pltpu.CompilerParams(vmem_limit_bytes=16 * MIB),
+        cost_estimate=pl.CostEstimate(
+            flops=8 * rows * width * units,
+            bytes_accessed=8 * width * units + 2 * rows * width,
+            transcendentals=0,
+        ),
+        name="down",
+    )(order, *pieces, weight)
+
+
+SWAP = [(0, 1), (1, 0)]
+
+
+def four_pieces(piece):
+    across = lax.ppermute(piece, "tensor", SWAP)
+    beside = lax.ppermute(piece, "node", SWAP)
+    return (piece, across, beside, lax.ppermute(across, "node", SWAP))
+
+
+def ring_shards(tokens, expert_ids, gate_weights, gate_weight, up_weight, down_weight):
+    owners = lax.axis_size("expert")
+    me = lax.axis_index("expert")
+    tensor, node = lax.axis_index("tensor"), lax.axis_index("node")
+    ring = [(i, (i + 1) % owners) for i in range(owners)]
+    order = jnp.stack(
+        [
+            tensor * 2 + node,
+            (1 - tensor) * 2 + node,
+            tensor * 2 + 1 - node,
+            (1 - tensor) * 2 + 1 - node,
+        ]
+    ).astype(jnp.int32)
+
+    def weight_at(expert):
+        return jnp.sum(jnp.where(expert_ids == expert, gate_weights, 0.0), axis=1)
+
+    shares = [weight_at(me)]
+    for s in range(1, owners):
+        shift = [(i, (i + s) % owners) for i in range(owners)]
+        column = weight_at(lax.rem(me + s, owners))
+        shares.append(lax.ppermute(column.reshape(1, -1), "expert", shift).reshape(-1))
+
+    blocks = [tokens]
+    for s in range(1, owners):
+        blocks.append(lax.ppermute(blocks[-1], "expert", ring))
+
+    def contribution(s):
+        hidden = gate_up(order, four_pieces(blocks[s]), gate_weight[0], up_weight[0])
+        result = down(order, four_pieces(hidden), down_weight[0])
+        share = shares[s][:, None]
+        return jnp.where(share != 0, share * result.astype(jnp.float32), 0.0)
+
+    own = contribution(0)
+    partial = None
+    for s in range(1, owners):
+        term = contribution(s)
+        if partial is not None:
+            term = term + partial.astype(jnp.float32)
+        partial = lax.ppermute(term.astype(jnp.bfloat16), "expert", ring)
+    return (own + partial.astype(jnp.float32)).astype(jnp.bfloat16)
+
+
+def shards(tokens, expert_ids, gate_weights, gate_weight, up_weight, down_weight):
+    experts = gate_weight.shape[0] * lax.axis_size("expert")
+    count_rows, top_slots = expert_ids.shape
+    capacity = 2 * count_rows * top_slots // experts
+    pairs = lax.axis_size("tensor") == 2 and lax.axis_size("node") == 2
+    whole_blocks = capacity >= count_rows and gate_weight.shape[0] == 1
+    body = ring_shards if pairs and whole_blocks else dispatch_shards
+    return body(tokens, expert_ids, gate_weights, gate_weight, up_weight, down_weight)
+
+
 def solution(mesh):
     placed = (
         P(("group", "expert"), ("tensor", "node")),

time: 311 us -> 118 us (0.38)
  blocking collectives: 166 us -> 0 us
  waiting for transfers between devices: 86.3 us -> 40.2 us
  Pallas kernels: 0 us -> 39.4 us
  matrix products: 19.8 us -> 0 us
  starting transfers between devices: 4.64 us -> 24.1 us
  between operations: 13.6 us -> 0.24 us
  other arithmetic: 8.74 us -> 2.1 us
    all_to_all x1 -> x0, blocking collectives: 166 us -> none  [shards(): lax.all_to_all(packed, 'expert', split_axis=0, concat_axis=0, tiled=True)]
    all_gather x2 -> x0, waiting for transfers between devices: 43.4 us -> none  [the longest x1 24 us: shards(): whole = lax.all_gather(tokens, ('tensor', 'node'), axis=1, tiled=True)]
    all_to_all x1 -> x0, waiting for transfers between devices: 42.2 us -> none  [shards(): lax.all_to_all(stacked, 'expert', split_axis=0, concat_axis=0, tiled=True)]
    ppermute x0 -> x33, waiting for transfers between devices: none -> 40.2 us  [the longest x8 18.3 us: four_pieces(): across = lax.ppermute(piece, 'tensor', SWAP)]
    pallas_call x0 -> x8, Pallas kernels: none -> 39.4 us  [the longest x4 30.1 us: gate_up(): pl.pallas_call(functools.partial(gate_up_kernel, splits), out_shape=jax.S...]
    ppermute x0 -> x33, starting transfers between devices: none -> 24.1 us  [the longest x8 8.6 us: four_pieces(): across = lax.ppermute(piece, 'tensor', SWAP)]
    dot_general x4 -> x0, matrix products: 19.8 us -> none  [the longest x1 8.16 us: shards(): jnp.dot(lax.all_gather(hidden, ('tensor', 'node'), axis=1, tiled=True), b...]
    unnamed x10 -> x18, local copies, waits for them, and re-layouts: 0.92 us -> 11.3 us
  transfers between devices with their start and end apart: 3 -> 33, of which waited for: 3 -> 12; matrix products, arithmetic and copies ran while one was open for 1% -> 1% of each run, Pallas kernels for 0% -> 34%
where the time goes in v1:
time: 118 us; the launch traced here: 117 us
  waiting for transfers between devices  40.2 us (34%)
  Pallas kernels  39.4 us (33%)
  starting transfers between devices  24.1 us (20%)
  local copies, waits for them, and re-layouts  11.3 us (10%)
  other arithmetic  2.1 us (2%)
    pallas_call x4, Pallas kernels, gate_up(): pl.pallas_call(functools.partial(gate_up_kernel, splits), out_shape=jax.S...  30.1 us
    ppermute x8, waiting for transfers between devices, four_pieces(): across = lax.ppermute(piece, 'tensor', SWAP)  18.3 us
    ppermute x3, waiting for transfers between devices, ring_shards(): blocks.append(lax.ppermute(blocks[-1], 'expert', ring))  15.4 us
    unnamed x18, local copies, waits for them, and re-layouts  11.3 us
    pallas_call x4, Pallas kernels, down(): pl.pallas_call(down_kernel, out_shape=jax.ShapeDtypeStruct((rows, width),...  9.31 us
    ppermute x8, starting transfers between devices, four_pieces(): across = lax.ppermute(piece, 'tensor', SWAP)  8.6 us
    ppermute x3, starting transfers between devices, ring_shards(): lax.ppermute(column.reshape(1, -1), 'expert', shift).reshape(-1)  6.27 us
    ppermute x3, starting transfers between devices, ring_shards(): partial = lax.ppermute(term.astype(jnp.bfloat16), 'expert', ring)  4.31 us
  transfers between devices with their start and end apart: 33, of which 12 were waited for; matrix products, arithmetic and copies ran while one was open for 1% of the time, Pallas kernels for 34%

profile of v1, /device:TPU:0, one launch (start us, length us, event | category | flops | bytes accessed | tf_op | source)
XLA Modules:
  0.0 117.3 jit_solution(11654921695511106157)
XLA Ops:
  0.0 3.0 %collective-permute-start.7 = (bf16[128,1792]{1,0:T(8,128)(2,1)}, bf16[128,1792]{1,0:T(8,128)(2,1)S(1)}, u32[]{:S(2)}, u32[]{:S(2)}) collective-permute-start(bf16[128,1792]{1,0:T(8,128)(2,1)} %refs_0_.1), channel_id=1, source_target_pairs={{0,4},{4,8},{8,12},{12,0},{1,5},{5,9},{9,13},{13,1},{2,6},{6,10},{... | collective-permute-start | bytes 1376264 | tf_op jit(solution)/shard_map/ppermute | solution.py:212
  3.0 12.8 %collective-permute-done.7.refs_0_ = bf16[128,1792]{1,0:T(8,128)(2,1)S(1)} collective-permute-done((bf16[128,1792]{1,0:T(8,128)(2,1)}, bf16[128,1792]{1,0:T(8,128)(2,1)S(1)}, u32[]{:S(2)}, u32[]{:S(2)}) %collective-permute-start.7) | collective-permute-done | bytes 458784 | tf_op jit(solution)/shard_map/ppermute | solution.py:212
  15.8 1.5 %collective-permute-start.24 = (bf16[128,1792]{1,0:T(8,128)(2,1)S(1)}, bf16[128,1792]{1,0:T(8,128)(2,1)S(1)}, u32[]{:S(2)}, u32[]{:S(2)}) collective-permute-start(bf16[128,1792]{1,0:T(8,128)(2,1)S(1)} %collective-permute-done.7.refs_0_), channel_id=1, source_target_pairs={{0,2},{2,0},{1,3},{3,1},{4,6},{6,4},{5,7},{7,5},{8,10},{10,8},{9,1... | collective-permute-start | bytes 1376264 | tf_op jit(solution)/shard_map/ppermute | solution.py:182
  17.3 10.2 %collective-permute-done.24.refs_1_ = bf16[128,1792]{1,0:T(8,128)(2,1)S(1)} collective-permute-done((bf16[128,1792]{1,0:T(8,128)(2,1)S(1)}, bf16[128,1792]{1,0:T(8,128)(2,1)S(1)}, u32[]{:S(2)}, u32[]{:S(2)}) %collective-permute-start.24) | collective-permute-done | bytes 458784 | tf_op jit(solution)/shard_map/ppermute | solution.py:182
  27.6 2.7 %collective-permute-done.8.refs_0_ = bf16[128,1792]{1,0:T(8,128)(2,1)S(1)} collective-permute-done((bf16[128,1792]{1,0:T(8,128)(2,1)S(1)}, bf16[128,1792]{1,0:T(8,128)(2,1)S(1)}, u32[]{:S(2)}, u32[]{:S(2)}) %collective-permute-start.8) | collective-permute-done | bytes 458784 | tf_op jit(solution)/shard_map/ppermute | solution.py:212
  31.1 2.8 %copy-done = bf16[1,448,7168]{2,1,0:T(8,128)(2,1)S(1)} copy-done((bf16[1,448,7168]{2,1,0:T(8,128)(2,1)S(1)}, bf16[1,448,7168]{2,1,0:T(8,128)(2,1)}, u32[]{:S(2)}) %copy-start) | copy-done | bytes 6422552
  33.9 2.8 %copy-done.2 = bf16[1,448,7168]{2,1,0:T(8,128)(2,1)S(1)} copy-done((bf16[1,448,7168]{2,1,0:T(8,128)(2,1)S(1)}, bf16[1,448,7168]{2,1,0:T(8,128)(2,1)}, u32[]{:S(2)}) %copy-start.2) | copy-done | bytes 6422552
  36.7 7.5 %gate_up.7.refs_0_ = bf16[128,448]{1,0:T(8,128)(2,1)S(1)} custom-call(s32[4]{0:T(128)S(1)} %pad_add_fusion.order_ref, bf16[128,1792]{1,0:T(8,128)(2,1)S(1)} %collective-permute-done.7.refs_0_, bf16[128,1792]{1,0:T(8,128)(2,1)S(1)} %collective-permute-done.24.refs_1_, bf16[128,1792]{1,0:T(8,128)(2,1)S(1)} %collective-permute-done.25.refs_2_, ...), custom_call_target="tpu_custom_call" | custom-call | flops 1644167168 | bytes 14680064 | tf_op jit(solution)/shard_map/gate_up/pallas_call | solution.py:117
  45.7 3.6 %collective-permute-done.27.refs_1_ = bf16[128,448]{1,0:T(8,128)(2,1)S(1)} collective-permute-done((bf16[128,448]{1,0:T(8,128)(2,1)S(1)}, bf16[128,448]{1,0:T(8,128)(2,1)S(1)}, u32[]{:S(2)}, u32[]{:S(2)}) %collective-permute-start.27) | collective-permute-done | bytes 114720 | tf_op jit(solution)/shard_map/ppermute | solution.py:182
  49.2 1.7 %collective-permute-done.23 = f32[1,128]{1,0:T(1,128)S(1)} collective-permute-done((f32[1,128]{1,0:T(1,128)S(1)}, f32[1,128]{1,0:T(1,128)S(1)}, u32[]{:S(2)}, u32[]{:S(2)}) %collective-permute-start.23) | collective-permute-done | bytes 544 | tf_op jit(solution)/shard_map/ppermute | solution.py:208
  52.2 2.8 %copy-done.4 = bf16[1,1792,1792]{2,1,0:T(8,128)(2,1)S(1)} copy-done((bf16[1,1792,1792]{2,1,0:T(8,128)(2,1)S(1)}, bf16[1,1792,1792]{2,1,0:T(8,128)(2,1)}, u32[]{:S(2)}) %copy-start.4) | copy-done | bytes 6422552
  55.0 2.3 %down.7 = bf16[128,1792]{1,0:T(8,128)(2,1)S(1)} custom-call(s32[4]{0:T(128)S(1)} %pad_add_fusion.order_ref, bf16[128,448]{1,0:T(8,128)(2,1)S(1)} %gate_up.7.refs_0_, bf16[128,448]{1,0:T(8,128)(2,1)S(1)} %collective-permute-done.27.refs_1_, bf16[128,448]{1,0:T(8,128)(2,1)S(1)} %collective-permute-done.28.refs_2_, ...), custom_call_target="tpu_custom_call" | custom-call | flops 822083584 | bytes 6881280 | tf_op jit(solution)/shard_map/down/pallas_call | solution.py:158
  57.7 2.8 %copy-done.3 = bf16[1,448,7168]{2,1,0:T(8,128)(2,1)S(1)} copy-done((bf16[1,448,7168]{2,1,0:T(8,128)(2,1)S(1)}, bf16[1,448,7168]{2,1,0:T(8,128)(2,1)}, u32[]{:S(2)}) %copy-start.3) | copy-done | bytes 6422552
  60.6 7.5 %gate_up.6.refs_0_ = bf16[128,448]{1,0:T(8,128)(2,1)S(1)} custom-call(s32[4]{0:T(128)S(1)} %pad_add_fusion.order_ref, bf16[128,1792]{1,0:T(8,128)(2,1)S(1)} %collective-permute-done.8.refs_0_, bf16[128,1792]{1,0:T(8,128)(2,1)S(1)} %collective-permute-done.17.refs_1_, bf16[128,1792]{1,0:T(8,128)(2,1)S(1)} %collective-permute-done.18.refs_2_, ...), custom_call_target="tpu_custom_call" | custom-call | flops 1644167168 | bytes 14680064 | tf_op jit(solution)/shard_map/gate_up/pallas_call | solution.py:117
  69.4 2.8 %collective-permute-start.16 = (f32[1,128]{1,0:T(1,128)S(1)}, f32[1,128]{1,0:T(1,128)S(1)}, u32[]{:S(2)}, u32[]{:S(2)}) collective-permute-start(f32[1,128]{1,0:T(1,128)S(1)} %bitcast.32), channel_id=1, source_target_pairs={{0,8},{4,12},{8,0},{12,4},{1,9},{5,13},{9,1},{13,5},{2,10},{6,14},... | collective-permute-start | bytes 1544 | tf_op jit(solution)/shard_map/ppermute | solution.py:208
  75.4 2.3 %down.6 = bf16[128,1792]{1,0:T(8,128)(2,1)S(1)} custom-call(s32[4]{0:T(128)S(1)} %pad_add_fusion.order_ref, bf16[128,448]{1,0:T(8,128)(2,1)S(1)} %gate_up.6.refs_0_, bf16[128,448]{1,0:T(8,128)(2,1)S(1)} %collective-permute-done.20.refs_1_, bf16[128,448]{1,0:T(8,128)(2,1)S(1)} %collective-permute-done.21.refs_2_, ...), custom_call_target="tpu_custom_call" | custom-call | flops 822083584 | bytes 6881280 | tf_op jit(solution)/shard_map/down/pallas_call | solution.py:158
  78.0 1.7 %collective-permute-start.31 = (bf16[128,1792]{1,0:T(8,128)(2,1)S(1)}, bf16[128,1792]{1,0:T(8,128)(2,1)S(1)}, u32[]{:S(2)}, u32[]{:S(2)}) collective-permute-start(bf16[128,1792]{1,0:T(8,128)(2,1)S(1)} %add_convert_fusion.2), channel_id=1, source_target_pairs={{0,4},{4,8},{8,12},{12,0},{1,5},{5,9},{9,13},{13,1},{2,6},{6,10},{... | collective-permute-start | bytes 1376264 | tf_op jit(solution)/shard_map/ppermute | solution.py:226
  79.7 7.5 %gate_up.5.refs_0_ = bf16[128,448]{1,0:T(8,128)(2,1)S(1)} custom-call(s32[4]{0:T(128)S(1)} %pad_add_fusion.order_ref, bf16[128,1792]{1,0:T(8,128)(2,1)S(1)} %collective-permute-done.9.refs_0_, bf16[128,1792]{1,0:T(8,128)(2,1)S(1)} %collective-permute-done.10.refs_1_, bf16[128,1792]{1,0:T(8,128)(2,1)S(1)} %collective-permute-done.11.refs_2_, ...), custom_call_target="tpu_custom_call" | custom-call | flops 1644167168 | bytes 14680064 | tf_op jit(solution)/shard_map/gate_up/pallas_call | solution.py:117
  88.1 3.4 %collective-permute-start.6 = (f32[1,128]{1,0:T(1,128)S(1)}, f32[1,128]{1,0:T(1,128)S(1)}, u32[]{:S(2)}, u32[]{:S(2)}) collective-permute-start(f32[1,128]{1,0:T(1,128)S(1)} %bitcast.31), channel_id=1, source_target_pairs={{0,12},{4,0},{8,4},{12,8},{1,13},{5,1},{9,5},{13,9},{2,14},{6,2},{... | collective-permute-start | bytes 1544 | tf_op jit(solution)/shard_map/ppermute | solution.py:208
  94.3 2.3 %down.5 = bf16[128,1792]{1,0:T(8,128)(2,1)S(1)} custom-call(s32[4]{0:T(128)S(1)} %pad_add_fusion.order_ref, bf16[128,448]{1,0:T(8,128)(2,1)S(1)} %gate_up.5.refs_0_, bf16[128,448]{1,0:T(8,128)(2,1)S(1)} %collective-permute-done.13.refs_1_, bf16[128,448]{1,0:T(8,128)(2,1)S(1)} %collective-permute-done.14.refs_2_, ...), custom_call_target="tpu_custom_call" | custom-call | flops 822083584 | bytes 6881280 | tf_op jit(solution)/shard_map/down/pallas_call | solution.py:158
  97.0 2.6 %collective-permute-start.32 = (bf16[128,1792]{1,0:T(8,128)(2,1)S(1)}, bf16[128,1792]{1,0:T(8,128)(2,1)S(1)}, u32[]{:S(2)}, u32[]{:S(2)}) collective-permute-start(bf16[128,1792]{1,0:T(8,128)(2,1)S(1)} %add_convert_fusion.1), channel_id=1, source_target_pairs={{0,4},{4,8},{8,12},{12,0},{1,5},{5,9},{9,13},{13,1},{2,6},{6,10},{... | collective-permute-start | bytes 1376264 | tf_op jit(solution)/shard_map/ppermute | solution.py:226
  99.6 7.5 %gate_up.4.refs_0_ = bf16[128,448]{1,0:T(8,128)(2,1)S(1)} custom-call(s32[4]{0:T(128)S(1)} %pad_add_fusion.order_ref, bf16[128,1792]{1,0:T(8,128)(2,1)S(1)} %copy-done.6, bf16[128,1792]{1,0:T(8,128)(2,1)S(1)} %collective-permute-done.refs_1_, bf16[128,1792]{1,0:T(8,128)(2,1)S(1)} %collective-permute-done.1.refs_2_, ...), custom_call_target="tpu_custom_call" | custom-call | flops 1644167168 | bytes 14680064 | tf_op jit(solution)/shard_map/gate_up/pallas_call | solution.py:117
  108.0 4.5 %collective-permute-done.3.refs_1_ = bf16[128,448]{1,0:T(8,128)(2,1)S(1)} collective-permute-done((bf16[128,448]{1,0:T(8,128)(2,1)S(1)}, bf16[128,448]{1,0:T(8,128)(2,1)S(1)}, u32[]{:S(2)}, u32[]{:S(2)}) %collective-permute-start.3) | collective-permute-done | bytes 114720 | tf_op jit(solution)/shard_map/ppermute | solution.py:182
  113.8 2.3 %down.4 = bf16[128,1792]{1,0:T(8,128)(2,1)S(1)} custom-call(s32[4]{0:T(128)S(1)} %pad_add_fusion.order_ref, bf16[128,448]{1,0:T(8,128)(2,1)S(1)} %gate_up.4.refs_0_, bf16[128,448]{1,0:T(8,128)(2,1)S(1)} %collective-permute-done.3.refs_1_, bf16[128,448]{1,0:T(8,128)(2,1)S(1)} %collective-permute-done.4.refs_2_, ...), custom_call_target="tpu_custom_call" | custom-call | flops 822083584 | bytes 6881280 | tf_op jit(solution)/shard_map/down/pallas_call | solution.py:158
  (78 shorter events, 16.0 us)
Async XLA Ops:
  0.0 15.8 %collective-permute-start.7 = (bf16[128,1792]{1,0:T(8,128)(2,1)}, bf16[128,1792]{1,0:T(8,128)(2,1)S(1)}, u32[]{:S(2)}, u32[]{:S(2)}) collective-permute-start(bf16[128,1792]{1,0:T(8,128)(2,1)} %refs_0_.1), channel_id=1, source_target_pairs={{0,4},{4,8},{8,12},{12,0},{1,5},{5,9},{9,13},{13,1},{2,6},{6,10},{... | collective-permute-start | bytes 1376264 | tf_op jit(solution)/shard_map/ppermute | solution.py:212
  15.8 11.7 %collective-permute-start.24 = (bf16[128,1792]{1,0:T(8,128)(2,1)S(1)}, bf16[128,1792]{1,0:T(8,128)(2,1)S(1)}, u32[]{:S(2)}, u32[]{:S(2)}) collective-permute-start(bf16[128,1792]{1,0:T(8,128)(2,1)S(1)} %collective-permute-done.7.refs_0_), channel_id=1, source_target_pairs={{0,2},{2,0},{1,3},{3,1},{4,6},{6,4},{5,7},{7,5},{8,10},{10,8},{9,1... | collective-permute-start | bytes 1376264 | tf_op jit(solution)/shard_map/ppermute | solution.py:182
  17.3 13.0 %collective-permute-start.8 = (bf16[128,1792]{1,0:T(8,128)(2,1)S(1)}, bf16[128,1792]{1,0:T(8,128)(2,1)S(1)}, u32[]{:S(2)}, u32[]{:S(2)}) collective-permute-start(bf16[128,1792]{1,0:T(8,128)(2,1)S(1)} %collective-permute-done.7.refs_0_), channel_id=1, source_target_pairs={{0,4},{4,8},{8,12},{12,0},{1,5},{5,9},{9,13},{13,1},{2,6},{6,10},{... | collective-permute-start | bytes 1376264 | tf_op jit(solution)/shard_map/ppermute | solution.py:212
  17.3 13.8 %collective-permute-start.25 = (bf16[128,1792]{1,0:T(8,128)(2,1)S(1)}, bf16[128,1792]{1,0:T(8,128)(2,1)S(1)}, u32[]{:S(2)}, u32[]{:S(2)}) collective-permute-start(bf16[128,1792]{1,0:T(8,128)(2,1)S(1)} %collective-permute-done.7.refs_0_), channel_id=1, source_target_pairs={{0,1},{1,0},{2,3},{3,2},{4,5},{5,4},{6,7},{7,6},{8,9},{9,8},{10,11... | collective-permute-start | bytes 1376264 | tf_op jit(solution)/shard_map/ppermute | solution.py:183
  30.2 20.7 %collective-permute-start.17 = (bf16[128,1792]{1,0:T(8,128)(2,1)S(1)}, bf16[128,1792]{1,0:T(8,128)(2,1)S(1)}, u32[]{:S(2)}, u32[]{:S(2)}) collective-permute-start(bf16[128,1792]{1,0:T(8,128)(2,1)S(1)} %collective-permute-done.8.refs_0_), channel_id=1, source_target_pairs={{0,2},{2,0},{1,3},{3,1},{4,6},{6,4},{5,7},{7,5},{8,10},{10,8},{9,1... | collective-permute-start | bytes 1376264 | tf_op jit(solution)/shard_map/ppermute | solution.py:182
  31.0 20.4 %collective-permute-start.9 = (bf16[128,1792]{1,0:T(8,128)(2,1)S(1)}, bf16[128,1792]{1,0:T(8,128)(2,1)S(1)}, u32[]{:S(2)}, u32[]{:S(2)}) collective-permute-start(bf16[128,1792]{1,0:T(8,128)(2,1)S(1)} %collective-permute-done.8.refs_0_), channel_id=1, source_target_pairs={{0,4},{4,8},{8,12},{12,0},{1,5},{5,9},{9,13},{13,1},{2,6},{6,10},{... | collective-permute-start | bytes 1376264 | tf_op jit(solution)/shard_map/ppermute | solution.py:212
  44.2 5.0 %collective-permute-start.27 = (bf16[128,448]{1,0:T(8,128)(2,1)S(1)}, bf16[128,448]{1,0:T(8,128)(2,1)S(1)}, u32[]{:S(2)}, u32[]{:S(2)}) collective-permute-start(bf16[128,448]{1,0:T(8,128)(2,1)S(1)} %gate_up.7.refs_0_), channel_id=1, source_target_pairs={{0,2},{2,0},{1,3},{3,1},{4,6},{6,4},{5,7},{7,5},{8,10},{10,8},{9,1... | collective-permute-start | bytes 344072 | tf_op jit(solution)/shard_map/ppermute | solution.py:182
  45.5 5.4 %collective-permute-start.23 = (f32[1,128]{1,0:T(1,128)S(1)}, f32[1,128]{1,0:T(1,128)S(1)}, u32[]{:S(2)}, u32[]{:S(2)}) collective-permute-start(f32[1,128]{1,0:T(1,128)S(1)} %bitcast.33), channel_id=1, source_target_pairs={{0,4},{4,8},{8,12},{12,0},{1,5},{5,9},{9,13},{13,1},{2,6},{6,10},{... | collective-permute-start | bytes 1544 | tf_op jit(solution)/shard_map/ppermute | solution.py:208
  45.6 6.6 %collective-permute-start.28 = (bf16[128,448]{1,0:T(8,128)(2,1)S(1)}, bf16[128,448]{1,0:T(8,128)(2,1)S(1)}, u32[]{:S(2)}, u32[]{:S(2)}) collective-permute-start(bf16[128,448]{1,0:T(8,128)(2,1)S(1)} %gate_up.7.refs_0_), channel_id=1, source_target_pairs={{0,1},{1,0},{2,3},{3,2},{4,5},{5,4},{6,7},{7,6},{8,9},{9,8},{10,11... | collective-permute-start | bytes 344072 | tf_op jit(solution)/shard_map/ppermute | solution.py:183
  50.9 6.8 %collective-permute-start.18 = (bf16[128,1792]{1,0:T(8,128)(2,1)S(1)}, bf16[128,1792]{1,0:T(8,128)(2,1)S(1)}, u32[]{:S(2)}, u32[]{:S(2)}) collective-permute-start(bf16[128,1792]{1,0:T(8,128)(2,1)S(1)} %collective-permute-done.8.refs_0_), channel_id=1, source_target_pairs={{0,1},{1,0},{2,3},{3,2},{4,5},{5,4},{6,7},{7,6},{8,9},{9,8},{10,11... | collective-permute-start | bytes 1376264 | tf_op jit(solution)/shard_map/ppermute | solution.py:183
  50.9 6.8 %collective-permute-start.19 = (bf16[128,1792]{1,0:T(8,128)(2,1)S(1)}, bf16[128,1792]{1,0:T(8,128)(2,1)S(1)}, u32[]{:S(2)}, u32[]{:S(2)}) collective-permute-start(bf16[128,1792]{1,0:T(8,128)(2,1)S(1)} %collective-permute-done.17.refs_1_), channel_id=1, source_target_pairs={{0,1},{1,0},{2,3},{3,2},{4,5},{5,4},{6,7},{7,6},{8,9},{9,8},{10,11... | collective-permute-start | bytes 1376264 | tf_op jit(solution)/shard_map/ppermute | solution.py:184
  51.4 22.9 %collective-permute-start.10 = (bf16[128,1792]{1,0:T(8,128)(2,1)S(1)}, bf16[128,1792]{1,0:T(8,128)(2,1)S(1)}, u32[]{:S(2)}, u32[]{:S(2)}) collective-permute-start(bf16[128,1792]{1,0:T(8,128)(2,1)S(1)} %collective-permute-done.9.refs_0_), channel_id=1, source_target_pairs={{0,2},{2,0},{1,3},{3,1},{4,6},{6,4},{5,7},{7,5},{8,10},{10,8},{9,1... | collective-permute-start | bytes 1376264 | tf_op jit(solution)/shard_map/ppermute | solution.py:182
  57.6 20.1 %collective-permute-start.30 = (bf16[128,1792]{1,0:T(8,128)(2,1)S(1)}, bf16[128,1792]{1,0:T(8,128)(2,1)S(1)}, u32[]{:S(2)}, u32[]{:S(2)}) collective-permute-start(bf16[128,1792]{1,0:T(8,128)(2,1)S(1)} %select_convert_fusion), channel_id=1, source_target_pairs={{0,4},{4,8},{8,12},{12,0},{1,5},{5,9},{9,13},{13,1},{2,6},{6,10},{... | collective-permute-start | bytes 1376264 | tf_op jit(solution)/shard_map/ppermute | solution.py:226
  68.1 5.8 %collective-permute-start.20 = (bf16[128,448]{1,0:T(8,128)(2,1)S(1)}, bf16[128,448]{1,0:T(8,128)(2,1)S(1)}, u32[]{:S(2)}, u32[]{:S(2)}) collective-permute-start(bf16[128,448]{1,0:T(8,128)(2,1)S(1)} %gate_up.6.refs_0_), channel_id=1, source_target_pairs={{0,2},{2,0},{1,3},{3,1},{4,6},{6,4},{5,7},{7,5},{8,10},{10,8},{9,1... | collective-permute-start | bytes 344072 | tf_op jit(solution)/shard_map/ppermute | solution.py:182
  72.2 21.1 %collective-permute-start = (bf16[128,1792]{1,0:T(8,128)(2,1)S(1)}, bf16[128,1792]{1,0:T(8,128)(2,1)S(1)}, u32[]{:S(2)}, u32[]{:S(2)}) collective-permute-start(bf16[128,1792]{1,0:T(8,128)(2,1)S(1)} %copy-done.6), channel_id=1, source_target_pairs={{0,2},{2,0},{1,3},{3,1},{4,6},{6,4},{5,7},{7,5},{8,10},{10,8},{9,1... | collective-permute-start | bytes 1376264 | tf_op jit(solution)/shard_map/ppermute | solution.py:182
  74.4 5.4 %collective-permute-start.11 = (bf16[128,1792]{1,0:T(8,128)(2,1)S(1)}, bf16[128,1792]{1,0:T(8,128)(2,1)S(1)}, u32[]{:S(2)}, u32[]{:S(2)}) collective-permute-start(bf16[128,1792]{1,0:T(8,128)(2,1)S(1)} %collective-permute-done.9.refs_0_), channel_id=1, source_target_pairs={{0,1},{1,0},{2,3},{3,2},{4,5},{5,4},{6,7},{7,6},{8,9},{9,8},{10,11... | collective-permute-start | bytes 1376264 | tf_op jit(solution)/shard_map/ppermute | solution.py:183
  75.2 4.5 %collective-permute-start.12 = (bf16[128,1792]{1,0:T(8,128)(2,1)S(1)}, bf16[128,1792]{1,0:T(8,128)(2,1)S(1)}, u32[]{:S(2)}, u32[]{:S(2)}) collective-permute-start(bf16[128,1792]{1,0:T(8,128)(2,1)S(1)} %collective-permute-done.10.refs_1_), channel_id=1, source_target_pairs={{0,1},{1,0},{2,3},{3,2},{4,5},{5,4},{6,7},{7,6},{8,9},{9,8},{10,11... | collective-permute-start | bytes 1376264 | tf_op jit(solution)/shard_map/ppermute | solution.py:184
  78.0 18.6 %collective-permute-start.31 = (bf16[128,1792]{1,0:T(8,128)(2,1)S(1)}, bf16[128,1792]{1,0:T(8,128)(2,1)S(1)}, u32[]{:S(2)}, u32[]{:S(2)}) collective-permute-start(bf16[128,1792]{1,0:T(8,128)(2,1)S(1)} %add_convert_fusion.2), channel_id=1, source_target_pairs={{0,4},{4,8},{8,12},{12,0},{1,5},{5,9},{9,13},{13,1},{2,6},{6,10},{... | collective-permute-start | bytes 1376264 | tf_op jit(solution)/shard_map/ppermute | solution.py:226
  87.3 5.6 %collective-permute-start.13 = (bf16[128,448]{1,0:T(8,128)(2,1)S(1)}, bf16[128,448]{1,0:T(8,128)(2,1)S(1)}, u32[]{:S(2)}, u32[]{:S(2)}) collective-permute-start(bf16[128,448]{1,0:T(8,128)(2,1)S(1)} %gate_up.5.refs_0_), channel_id=1, source_target_pairs={{0,2},{2,0},{1,3},{3,1},{4,6},{6,4},{5,7},{7,5},{8,10},{10,8},{9,1... | collective-permute-start | bytes 344072 | tf_op jit(solution)/shard_map/ppermute | solution.py:182
  88.1 4.7 %collective-permute-start.6 = (f32[1,128]{1,0:T(1,128)S(1)}, f32[1,128]{1,0:T(1,128)S(1)}, u32[]{:S(2)}, u32[]{:S(2)}) collective-permute-start(f32[1,128]{1,0:T(1,128)S(1)} %bitcast.31), channel_id=1, source_target_pairs={{0,12},{4,0},{8,4},{12,8},{1,13},{5,1},{9,5},{13,9},{2,14},{6,2},{... | collective-permute-start | bytes 1544 | tf_op jit(solution)/shard_map/ppermute | solution.py:208
  91.5 8.1 %collective-permute-start.1 = (bf16[128,1792]{1,0:T(8,128)(2,1)S(1)}, bf16[128,1792]{1,0:T(8,128)(2,1)S(1)}, u32[]{:S(2)}, u32[]{:S(2)}) collective-permute-start(bf16[128,1792]{1,0:T(8,128)(2,1)S(1)} %copy-done.6), channel_id=1, source_target_pairs={{0,1},{1,0},{2,3},{3,2},{4,5},{5,4},{6,7},{7,6},{8,9},{9,8},{10,11... | collective-permute-start | bytes 1376264 | tf_op jit(solution)/shard_map/ppermute | solution.py:183
  93.3 6.3 %collective-permute-start.2 = (bf16[128,1792]{1,0:T(8,128)(2,1)S(1)}, bf16[128,1792]{1,0:T(8,128)(2,1)S(1)}, u32[]{:S(2)}, u32[]{:S(2)}) collective-permute-start(bf16[128,1792]{1,0:T(8,128)(2,1)S(1)} %collective-permute-done.refs_1_), channel_id=1, source_target_pairs={{0,1},{1,0},{2,3},{3,2},{4,5},{5,4},{6,7},{7,6},{8,9},{9,8},{10,11... | collective-permute-start | bytes 1376264 | tf_op jit(solution)/shard_map/ppermute | solution.py:184
  97.0 19.2 %collective-permute-start.32 = (bf16[128,1792]{1,0:T(8,128)(2,1)S(1)}, bf16[128,1792]{1,0:T(8,128)(2,1)S(1)}, u32[]{:S(2)}, u32[]{:S(2)}) collective-permute-start(bf16[128,1792]{1,0:T(8,128)(2,1)S(1)} %add_convert_fusion.1), channel_id=1, source_target_pairs={{0,4},{4,8},{8,12},{12,0},{1,5},{5,9},{9,13},{13,1},{2,6},{6,10},{... | collective-permute-start | bytes 1376264 | tf_op jit(solution)/shard_map/ppermute | solution.py:226
  107.2 5.3 %collective-permute-start.3 = (bf16[128,448]{1,0:T(8,128)(2,1)S(1)}, bf16[128,448]{1,0:T(8,128)(2,1)S(1)}, u32[]{:S(2)}, u32[]{:S(2)}) collective-permute-start(bf16[128,448]{1,0:T(8,128)(2,1)S(1)} %gate_up.4.refs_0_), channel_id=1, source_target_pairs={{0,2},{2,0},{1,3},{3,1},{4,6},{6,4},{5,7},{7,5},{8,10},{10,8},{9,1... | collective-permute-start | bytes 344072 | tf_op jit(solution)/shard_map/ppermute | solution.py:182
  (18 other events, 93.4 us)

commit v2 on v0

--- a/solution.py
+++ b/solution.py
@@ -1,7 +1,13 @@
+import functools
+
 import jax
 import jax.numpy as jnp
 from jax import lax
+from jax.experimental import pallas as pl
+from jax.experimental.pallas import tpu as pltpu
 from jax.sharding import PartitionSpec as P
+
+MIB = 1 << 20
 
 
 def route_positions(expert_ids, experts):
@@ -31,7 +37,7 @@
     return jnp.take(padded, slot_table, axis=0).reshape(experts, capacity, rows.shape[1])
 
 
-def shards(tokens, expert_ids, gate_weights, gate_weight, up_weight, down_weight):
+def dispatch_shards(tokens, expert_ids, gate_weights, gate_weight, up_weight, down_weight):
     owners = lax.axis_size("expert")
     local_experts = gate_weight.shape[0]
     experts = local_experts * owners
@@ -68,6 +74,220 @@
     return mixed.astype(jnp.bfloat16)
 
 
+ROWS = (((1,), (1,)), ((), ()))
+
+
+def in_hbm(array):
+    return pltpu.with_memory_space_constraint(array, pltpu.HBM)
+
+
+def in_vmem(array):
+    return pltpu.with_memory_space_constraint(array, pltpu.VMEM)
+
+
+def load_kernel(count, *refs):
+    sources, targets, sems = refs[:count], refs[-count - 1 : -1], refs[-1]
+    refs[-count - 2][...] = jnp.zeros_like(refs[-count - 2])
+    copies = [
+        pltpu.make_async_copy(source, target, sems.at[i])
+        for i, (source, target) in enumerate(zip(sources, targets))
+    ]
+    for copy in copies:
+        copy.start()
+    for copy in copies:
+        copy.wait()
+
+
+def load(arrays, *after):
+    count = len(arrays)
+    return pl.pallas_call(
+        functools.partial(load_kernel, count),
+        out_shape=[jax.ShapeDtypeStruct((8, 128), jnp.float32)]
+        + [pltpu.VMEM(a.shape, a.dtype) for a in arrays],
+        in_specs=[pl.BlockSpec(memory_space=pltpu.HBM)] * count
+        + [pl.BlockSpec(memory_space=pl.ANY)] * len(after),
+        out_specs=[pl.BlockSpec(memory_space=pltpu.VMEM)] * (count + 1),
+        scratch_shapes=[pltpu.SemaphoreType.DMA((count,))],
+        compiler_params=pltpu.CompilerParams(vmem_limit_bytes=1 * MIB),
+        cost_estimate=pl.CostEstimate(
+            flops=0, bytes_accessed=2 * sum(a.size * 2 for a in arrays), transcendentals=0
+        ),
+        name="load",
+    )(*[in_hbm(a) for a in arrays], *after)
+
+
+def gate_up_kernel(order_ref, *refs):
+    pieces = refs[:4]
+    gate_ref, up_ref = refs[4:6]
+    out_ref = refs[-1]
+    width = pieces[0].shape[1]
+    gate = up = 0.0
+    for j, piece in enumerate(pieces):
+        columns = pl.ds(pl.multiple_of(order_ref[j] * width, width), width)
+        rows = piece[...]
+        gate += lax.dot_general(
+            rows, gate_ref[:, columns], ROWS, preferred_element_type=jnp.float32
+        )
+        up += lax.dot_general(rows, up_ref[:, columns], ROWS, preferred_element_type=jnp.float32)
+    out_ref[...] = (gate / (1.0 + jnp.exp(-gate)) * up).astype(out_ref.dtype)
+
+
+def gate_up(order, pieces, gate_weight, up_weight, *after):
+    rows, width = pieces[0].shape
+    units = gate_weight.shape[0]
+    whole = pl.BlockSpec(memory_space=pltpu.VMEM)
+    apart = pl.BlockSpec(memory_space=pl.ANY)
+    return pl.pallas_call(
+        gate_up_kernel,
+        out_shape=jax.ShapeDtypeStruct((rows, units), jnp.bfloat16),
+        in_specs=[pl.BlockSpec(memory_space=pltpu.SMEM)] + [whole] * 6 + [apart] * len(after),
+        out_specs=whole,
+        compiler_params=pltpu.CompilerParams(vmem_limit_bytes=4 * MIB),
+        cost_estimate=pl.CostEstimate(
+            flops=16 * rows * width * units,
+            bytes_accessed=16 * width * units + 8 * rows * width,
+            transcendentals=rows * units,
+        ),
+        name="gate_up",
+    )(order, *pieces, in_vmem(gate_weight), in_vmem(up_weight), *after)
+
+
+def down_kernel(order_ref, *refs):
+    pieces = refs[:4]
+    weight_ref = refs[4]
+    out_ref, blocks, sems = refs[-3:]
+    units = pieces[0].shape[1]
+    copies = []
+    for j in range(4):
+        rows = pl.ds(pl.multiple_of(order_ref[j] * units, units), units)
+        copies.append(pltpu.make_async_copy(weight_ref.at[rows, :], blocks.at[j], sems.at[j]))
+    for copy in copies:
+        copy.start()
+    total = 0.0
+    for j, piece in enumerate(pieces):
+        copies[j].wait()
+        total += jnp.dot(piece[...], blocks[j], preferred_element_type=jnp.float32)
+    out_ref[...] = total.astype(out_ref.dtype)
+
+
+def down_kernel(order_ref, *refs):
+    pieces = refs[:4]
+    weight_ref, out_ref = refs[4:]
+    units = pieces[0].shape[1]
+    total = 0.0
+    for j, piece in enumerate(pieces):
+        block = weight_ref[pl.ds(pl.multiple_of(order_ref[j] * units, units), units), :]
+        total += jnp.dot(piece[...], block, preferred_element_type=jnp.float32)
+    out_ref[...] = total.astype(out_ref.dtype)
+
+
+def down(order, pieces, weight):
+    rows, units = pieces[0].shape
+    width = weight.shape[1]
+    whole = pl.BlockSpec(memory_space=pltpu.VMEM)
+    return pl.pallas_call(
+        down_kernel,
+        out_shape=jax.ShapeDtypeStruct((rows, width), jnp.bfloat16),
+        in_specs=[pl.BlockSpec(memory_space=pltpu.SMEM)] + [whole] * 5,
+        out_specs=whole,
+        compiler_params=pltpu.CompilerParams(vmem_limit_bytes=4 * MIB),
+        cost_estimate=pl.CostEstimate(
+            flops=8 * rows * width * units,
+            bytes_accessed=8 * width * units + 2 * rows * width,
+            transcendentals=0,
+        ),
+        name="down",
+    )(order, *pieces, in_vmem(weight))
+
+
+SWAP = [(0, 1), (1, 0)]
+
+
+def after(array, *others):
+    return lax.optimization_barrier((array, *others))[0]
+
+
+def swap(array, axis, what):
+    with jax.named_scope(what):
+        return lax.ppermute(array, axis, SWAP)
+
+
+def ring_shards(tokens, expert_ids, gate_weights, gate_weight, up_weight, down_weight):
+    owners = lax.axis_size("expert")
+    me = lax.axis_index("expert")
+    tensor, node = lax.axis_index("tensor"), lax.axis_index("node")
+    ring = [(i, (i + 1) % owners) for i in range(owners)]
+    order = jnp.stack(
+        [
+            tensor * 2 + node,
+            (1 - tensor) * 2 + node,
+            tensor * 2 + 1 - node,
+            (1 - tensor) * 2 + 1 - node,
+        ]
+    ).astype(jnp.int32)
+
+    named = expert_ids[None, :, :] == jnp.arange(owners, dtype=jnp.int32)[:, None, None]
+    dense = jnp.sum(jnp.where(named, gate_weights[None, :, :], 0.0), axis=2)
+    mine = jnp.arange(owners, dtype=jnp.int32)[:, None] == me
+
+    def onward(array, what, places=1):
+        shift = [(i, (i + places) % owners) for i in range(owners)]
+        with jax.named_scope(what):
+            return lax.ppermute(array, "expert", shift)
+
+    def quarters(own, beyond, what):
+        return (
+            own,
+            beyond,
+            swap(own, "node", what + "_c"),
+            swap(beyond, "node", what + "_xc"),
+        )
+
+    blocks, across, hidden = [tokens], [swap(tokens, "tensor", "tokens0_x")], []
+    blocks.append(onward(tokens, "tokens1_z"))
+    shares = [dense] + [onward(dense, f"share{s}_z", s) for s in range(1, owners)]
+    gate = up = out = None
+    for s in range(1, owners):
+        known = [across[s - 1], *shares[1:]] if s == 1 else [across[s - 1], hidden[s - 2]]
+        across.append(swap(after(blocks[s], *known), "tensor", f"tokens{s}_x"))
+        if s + 1 < owners:
+            onto = after(blocks[s], *known)
+            blocks.append(onward(onto, f"tokens{s + 1}_z"))
+        k = s - 1
+        own, beyond = after(blocks[k], *known, blocks[s]), after(across[k], *known, blocks[s])
+        if s == 1:
+            gate, up, out = after(gate_weight[0]), after(up_weight[0]), after(down_weight[0])
+        hidden.append(gate_up(order, quarters(own, beyond, f"tokens{k}"), gate, up))
+        across[s] = after(across[s], hidden[k])
+    k = owners - 1
+    hidden.append(gate_up(order, quarters(blocks[k], across[k], f"tokens{k}"), gate, up))
+
+    def contribution(s):
+        own = after(hidden[s], across[-1]) if s == 0 else hidden[s]
+        beyond = swap(own, "tensor", f"hidden{s}_x")
+        result = down(order, quarters(own, beyond, f"hidden{s}"), out)
+        share = jnp.sum(jnp.where(mine, shares[s], 0.0), axis=0)[:, None]
+        return jnp.where(share != 0, share * result.astype(jnp.float32), 0.0)
+
+    partial = None
+    for s in range(1, owners):
+        term = contribution(s)
+        if partial is not None:
+            term = term + partial.astype(jnp.float32)
+        partial = onward(term.astype(jnp.bfloat16), f"sum{s}_z")
+    return (contribution(0) + partial.astype(jnp.float32)).astype(jnp.bfloat16)
+
+
+def shards(tokens, expert_ids, gate_weights, gate_weight, up_weight, down_weight):
+    experts = gate_weight.shape[0] * lax.axis_size("expert")
+    count_rows, top_slots = expert_ids.shape
+    capacity = 2 * count_rows * top_slots // experts
+    pairs = lax.axis_size("tensor") == 2 and lax.axis_size("node") == 2
+    whole_blocks = capacity >= count_rows and gate_weight.shape[0] == 1
+    body = ring_shards if pairs and whole_blocks else dispatch_shards
+    return body(tokens, expert_ids, gate_weights, gate_weight, up_weight, down_weight)
+
+
 def solution(mesh):
     placed = (
         P(("group", "expert"), ("tensor", "node")),

time: 311 us -> 99.5 us (0.32)
  blocking collectives: 166 us -> 0 us
  waiting for transfers between devices: 86.3 us -> 40.6 us
  Pallas kernels: 0 us -> 23.9 us
  matrix products: 19.8 us -> 0 us
  starting transfers between devices: 4.64 us -> 19.3 us
  between operations: 13.6 us -> 0.27 us
  other arithmetic: 8.74 us -> 2.87 us
    all_to_all x1 -> x0, blocking collectives: 166 us -> none  [shards(): lax.all_to_all(packed, 'expert', split_axis=0, concat_axis=0, tiled=True)]
    all_gather x2 -> x0, waiting for transfers between devices: 43.4 us -> none  [the longest x1 24 us: shards(): whole = lax.all_gather(tokens, ('tensor', 'node'), axis=1, tiled=True)]
    all_to_all x1 -> x0, waiting for transfers between devices: 42.2 us -> none  [shards(): lax.all_to_all(stacked, 'expert', split_axis=0, concat_axis=0, tiled=True)]
    ppermute x0 -> x33, waiting for transfers between devices: none -> 40.6 us  [the longest x24 26.4 us: swap(): return lax.ppermute(array, axis, SWAP)]
    pallas_call x0 -> x8, Pallas kernels: none -> 23.9 us  [the longest x4 17.2 us: gate_up(): pl.pallas_call(gate_up_kernel, out_shape=jax.ShapeDtypeStruct((rows, unit...]
    dot_general x4 -> x0, matrix products: 19.8 us -> none  [the longest x1 8.16 us: shards(): jnp.dot(lax.all_gather(hidden, ('tensor', 'node'), axis=1, tiled=True), b...]
    ppermute x0 -> x33, starting transfers between devices: none -> 19.3 us  [the longest x9 9.67 us: onward(): return lax.ppermute(array, 'expert', shift)]
    unnamed x10 -> x16, local copies, waits for them, and re-layouts: 0.92 us -> 12.3 us
  transfers between devices with their start and end apart: 3 -> 33, of which waited for: 3 -> 14; matrix products, arithmetic and copies ran while one was open for 1% -> 1% of each run, Pallas kernels for 0% -> 24%
where the time goes in v2:
time: 99.5 us; the launch traced here: 99.2 us
  waiting for transfers between devices  40.6 us (41%)
  Pallas kernels  23.9 us (24%)
  starting transfers between devices  19.3 us (19%)
  local copies, waits for them, and re-layouts  12.3 us (12%)
  other arithmetic  2.87 us (3%)
    ppermute x24, waiting for transfers between devices, swap(): return lax.ppermute(array, axis, SWAP)  26.4 us
    pallas_call x4, Pallas kernels, gate_up(): pl.pallas_call(gate_up_kernel, out_shape=jax.ShapeDtypeStruct((rows, unit...  17.2 us
    ppermute x9, waiting for transfers between devices, onward(): return lax.ppermute(array, 'expert', shift)  14.2 us
    unnamed x16, local copies, waits for them, and re-layouts  12.3 us
    ppermute x9, starting transfers between devices, onward(): return lax.ppermute(array, 'expert', shift)  9.67 us
    ppermute x24, starting transfers between devices, swap(): return lax.ppermute(array, axis, SWAP)  9.63 us
    pallas_call x4, Pallas kernels, down(): pl.pallas_call(down_kernel, out_shape=jax.ShapeDtypeStruct((rows, width),...  6.66 us
  transfers between devices with their start and end apart: 33, of which 14 were waited for; matrix products, arithmetic and copies ran while one was open for 1% of the time, Pallas kernels for 24%

profile of v2, /device:TPU:0, one launch (start us, length us, event | category | flops | bytes accessed | tf_op | source)
XLA Modules:
  0.0 99.2 jit_solution(13940590540071438770)
XLA Ops:
  0.0 3.0 %collective-permute-start.4 = (bf16[128,1792]{1,0:T(8,128)(2,1)}, bf16[128,1792]{1,0:T(8,128)(2,1)S(1)}, u32[]{:S(2)}, u32[]{:S(2)}) collective-permute-start(bf16[128,1792]{1,0:T(8,128)(2,1)} %refs_0_), channel_id=1, source_target_pairs={{0,4},{4,8},{8,12},{12,0},{1,5},{5,9},{9,13},{13,1},{2,6},{6,10},{... | collective-permute-start | bytes 1376264 | tf_op jit(solution)/shard_map/tokens1_z/ppermute | solution.py:236
  3.0 1.5 %collective-permute-start = (bf16[128,1792]{1,0:T(8,128)(2,1)}, bf16[128,1792]{1,0:T(8,128)(2,1)S(1)}, u32[]{:S(2)}, u32[]{:S(2)}) collective-permute-start(bf16[128,1792]{1,0:T(8,128)(2,1)} %refs_0_), channel_id=1, source_target_pairs={{0,2},{2,0},{1,3},{3,1},{4,6},{6,4},{5,7},{7,5},{8,10},{10,8},{9,1... | collective-permute-start | bytes 1376264 | tf_op jit(solution)/shard_map/tokens0_x/ppermute | solution.py:212
  5.2 1.6 %collective-permute-start.1 = (f32[4,128]{1,0:T(4,128)S(1)}, f32[4,128]{1,0:T(4,128)S(1)}, u32[]{:S(2)}, u32[]{:S(2)}) collective-permute-start(f32[4,128]{1,0:T(4,128)S(1)} %select_reduce_fusion), channel_id=1, source_target_pairs={{0,4},{4,8},{8,12},{12,0},{1,5},{5,9},{9,13},{13,1},{2,6},{6,10},{... | collective-permute-start | bytes 6152 | tf_op jit(solution)/shard_map/share1_z/ppermute | solution.py:236
  8.0 2.7 %collective-permute-start.3 = (f32[4,128]{1,0:T(4,128)S(1)}, f32[4,128]{1,0:T(4,128)S(1)}, u32[]{:S(2)}, u32[]{:S(2)}) collective-permute-start(f32[4,128]{1,0:T(4,128)S(1)} %select_reduce_fusion), channel_id=1, source_target_pairs={{0,12},{4,0},{8,4},{12,8},{1,13},{5,1},{9,5},{13,9},{2,14},{6,2},{... | collective-permute-start | bytes 6152 | tf_op jit(solution)/shard_map/share3_z/ppermute | solution.py:236
  10.7 5.2 %collective-permute-done.1 = f32[4,128]{1,0:T(4,128)S(1)} collective-permute-done((f32[4,128]{1,0:T(4,128)S(1)}, f32[4,128]{1,0:T(4,128)S(1)}, u32[]{:S(2)}, u32[]{:S(2)}) %collective-permute-start.1) | collective-permute-done | bytes 2080 | tf_op jit(solution)/shard_map/share1_z/ppermute | solution.py:236
  16.5 1.5 %collective-permute-start.8 = (bf16[128,1792]{1,0:T(8,128)(2,1)S(1)}, bf16[128,1792]{1,0:T(8,128)(2,1)S(1)}, u32[]{:S(2)}, u32[]{:S(2)}) collective-permute-start(bf16[128,1792]{1,0:T(8,128)(2,1)S(1)} %collective-permute-done.4.refs_0_), channel_id=1, source_target_pairs={{0,2},{2,0},{1,3},{3,1},{4,6},{6,4},{5,7},{7,5},{8,10},{10,8},{9,1... | collective-permute-start | bytes 1376264 | tf_op jit(solution)/shard_map/tokens1_x/ppermute | solution.py:212
  18.9 2.8 %copy-done = bf16[1,448,7168]{2,1,0:T(8,128)(2,1)S(1)} copy-done((bf16[1,448,7168]{2,1,0:T(8,128)(2,1)S(1)}, bf16[1,448,7168]{2,1,0:T(8,128)(2,1)}, u32[]{:S(2)}) %copy-start) | copy-done | bytes 6422552
  21.7 2.8 %copy-done.3 = bf16[1,448,7168]{2,1,0:T(8,128)(2,1)S(1)} copy-done((bf16[1,448,7168]{2,1,0:T(8,128)(2,1)S(1)}, bf16[1,448,7168]{2,1,0:T(8,128)(2,1)}, u32[]{:S(2)}) %copy-start.3) | copy-done | bytes 6422552
  25.5 4.3 %gate_up.4.refs_0_ = bf16[128,448]{1,0:T(8,128)(2,1)S(1)} custom-call(s32[4]{0:T(128)S(1)} %pad_add_fusion.order_ref, bf16[128,1792]{1,0:T(8,128)(2,1)S(1)} %copy-done.7, bf16[128,1792]{1,0:T(8,128)(2,1)S(1)} %collective-permute-done.refs_1_, bf16[128,1792]{1,0:T(8,128)(2,1)S(1)} %collective-permute-done.5.refs_2_, ...), custom_call_target="tpu_custom_call" | custom-call | flops 1644167168 | bytes 14680064 | tf_op jit(solution)/shard_map/gate_up/pallas_call | solution.py:140
  29.9 2.2 %collective-permute-done.7.refs_0_ = bf16[128,1792]{1,0:T(8,128)(2,1)S(1)} collective-permute-done((bf16[128,1792]{1,0:T(8,128)(2,1)S(1)}, bf16[128,1792]{1,0:T(8,128)(2,1)S(1)}, u32[]{:S(2)}, u32[]{:S(2)}) %collective-permute-start.7) | collective-permute-done | bytes 458784 | tf_op jit(solution)/shard_map/tokens2_z/ppermute | solution.py:236
  34.5 2.8 %copy-done.1 = bf16[1,448,7168]{2,1,0:T(8,128)(2,1)S(1)} copy-done((bf16[1,448,7168]{2,1,0:T(8,128)(2,1)S(1)}, bf16[1,448,7168]{2,1,0:T(8,128)(2,1)}, u32[]{:S(2)}) %copy-start.1) | copy-done | bytes 6422552
  37.3 2.8 %copy-done.4 = bf16[1,448,7168]{2,1,0:T(8,128)(2,1)S(1)} copy-done((bf16[1,448,7168]{2,1,0:T(8,128)(2,1)S(1)}, bf16[1,448,7168]{2,1,0:T(8,128)(2,1)}, u32[]{:S(2)}) %copy-start.4) | copy-done | bytes 6422552
  40.2 4.3 %gate_up.5.refs_0_ = bf16[128,448]{1,0:T(8,128)(2,1)S(1)} custom-call(s32[4]{0:T(128)S(1)} %pad_add_fusion.order_ref, bf16[128,1792]{1,0:T(8,128)(2,1)S(1)} %collective-permute-done.4.refs_0_, bf16[128,1792]{1,0:T(8,128)(2,1)S(1)} %collective-permute-done.8.refs_1_, bf16[128,1792]{1,0:T(8,128)(2,1)S(1)} %collective-permute-done.11.refs_2_, ...), custom_call_target="tpu_custom_call" | custom-call | flops 1644167168 | bytes 14680064 | tf_op jit(solution)/shard_map/gate_up/pallas_call | solution.py:140
  45.2 4.9 %collective-permute-done.27.refs_1_ = bf16[128,448]{1,0:T(8,128)(2,1)S(1)} collective-permute-done((bf16[128,448]{1,0:T(8,128)(2,1)S(1)}, bf16[128,448]{1,0:T(8,128)(2,1)S(1)}, u32[]{:S(2)}, u32[]{:S(2)}) %collective-permute-start.27) | collective-permute-done | bytes 114720 | tf_op jit(solution)/shard_map/hidden1_x/ppermute | solution.py:212
  51.5 1.7 %down.7 = bf16[128,1792]{1,0:T(8,128)(2,1)S(1)} custom-call(s32[4]{0:T(128)S(1)} %pad_add_fusion.order_ref, bf16[128,448]{1,0:T(8,128)(2,1)S(1)} %gate_up.5.refs_0_, bf16[128,448]{1,0:T(8,128)(2,1)S(1)} %collective-permute-done.27.refs_1_, bf16[128,448]{1,0:T(8,128)(2,1)S(1)} %collective-permute-done.28.refs_2_, ...), custom_call_target="tpu_custom_call" | custom-call | flops 822083584 | bytes 6881280 | tf_op jit(solution)/shard_map/down/pallas_call | solution.py:188
  53.7 4.3 %gate_up.6.refs_0_ = bf16[128,448]{1,0:T(8,128)(2,1)S(1)} custom-call(s32[4]{0:T(128)S(1)} %pad_add_fusion.order_ref, bf16[128,1792]{1,0:T(8,128)(2,1)S(1)} %collective-permute-done.7.refs_0_, bf16[128,1792]{1,0:T(8,128)(2,1)S(1)} %collective-permute-done.10.refs_1_, bf16[128,1792]{1,0:T(8,128)(2,1)S(1)} %collective-permute-done.14.refs_2_, ...), custom_call_target="tpu_custom_call" | custom-call | flops 1644167168 | bytes 14680064 | tf_op jit(solution)/shard_map/gate_up/pallas_call | solution.py:140
  59.4 7.0 %collective-permute-done.24.refs_1_ = bf16[128,448]{1,0:T(8,128)(2,1)S(1)} collective-permute-done((bf16[128,448]{1,0:T(8,128)(2,1)S(1)}, bf16[128,448]{1,0:T(8,128)(2,1)S(1)}, u32[]{:S(2)}, u32[]{:S(2)}) %collective-permute-start.24) | collective-permute-done | bytes 114720 | tf_op jit(solution)/shard_map/hidden2_x/ppermute | solution.py:212
  67.8 1.7 %down.6 = bf16[128,1792]{1,0:T(8,128)(2,1)S(1)} custom-call(s32[4]{0:T(128)S(1)} %pad_add_fusion.order_ref, bf16[128,448]{1,0:T(8,128)(2,1)S(1)} %gate_up.6.refs_0_, bf16[128,448]{1,0:T(8,128)(2,1)S(1)} %collective-permute-done.24.refs_1_, bf16[128,448]{1,0:T(8,128)(2,1)S(1)} %collective-permute-done.25.refs_2_, ...), custom_call_target="tpu_custom_call" | custom-call | flops 822083584 | bytes 6881280 | tf_op jit(solution)/shard_map/down/pallas_call | solution.py:188
  69.9 4.3 %gate_up.7.refs_0_ = bf16[128,448]{1,0:T(8,128)(2,1)S(1)} custom-call(s32[4]{0:T(128)S(1)} %pad_add_fusion.order_ref, bf16[128,1792]{1,0:T(8,128)(2,1)S(1)} %collective-permute-done.9.refs_0_, bf16[128,1792]{1,0:T(8,128)(2,1)S(1)} %collective-permute-done.13.refs_1_, bf16[128,1792]{1,0:T(8,128)(2,1)S(1)} %collective-permute-done.19.refs_2_, ...), custom_call_target="tpu_custom_call" | custom-call | flops 1644167168 | bytes 14680064 | tf_op jit(solution)/shard_map/gate_up/pallas_call | solution.py:140
  74.8 5.0 %collective-permute-done.21.refs_1_ = bf16[128,448]{1,0:T(8,128)(2,1)S(1)} collective-permute-done((bf16[128,448]{1,0:T(8,128)(2,1)S(1)}, bf16[128,448]{1,0:T(8,128)(2,1)S(1)}, u32[]{:S(2)}, u32[]{:S(2)}) %collective-permute-start.21) | collective-permute-done | bytes 114720 | tf_op jit(solution)/shard_map/hidden3_x/ppermute | solution.py:212
  81.2 1.7 %down.5 = bf16[128,1792]{1,0:T(8,128)(2,1)S(1)} custom-call(s32[4]{0:T(128)S(1)} %pad_add_fusion.order_ref, bf16[128,448]{1,0:T(8,128)(2,1)S(1)} %gate_up.7.refs_0_, bf16[128,448]{1,0:T(8,128)(2,1)S(1)} %collective-permute-done.21.refs_1_, bf16[128,448]{1,0:T(8,128)(2,1)S(1)} %collective-permute-done.22.refs_2_, ...), custom_call_target="tpu_custom_call" | custom-call | flops 822083584 | bytes 6881280 | tf_op jit(solution)/shard_map/down/pallas_call | solution.py:188
  85.2 4.4 %collective-permute-done.16.refs_1_ = bf16[128,448]{1,0:T(8,128)(2,1)S(1)} collective-permute-done((bf16[128,448]{1,0:T(8,128)(2,1)S(1)}, bf16[128,448]{1,0:T(8,128)(2,1)S(1)}, u32[]{:S(2)}, u32[]{:S(2)}) %collective-permute-start.16) | collective-permute-done | bytes 114720 | tf_op jit(solution)/shard_map/hidden0_x/ppermute | solution.py:212
  91.0 1.7 %down.4 = bf16[128,1792]{1,0:T(8,128)(2,1)S(1)} custom-call(s32[4]{0:T(128)S(1)} %pad_add_fusion.order_ref, bf16[128,448]{1,0:T(8,128)(2,1)S(1)} %gate_up.4.refs_0_, bf16[128,448]{1,0:T(8,128)(2,1)S(1)} %collective-permute-done.16.refs_1_, bf16[128,448]{1,0:T(8,128)(2,1)S(1)} %collective-permute-done.17.refs_2_, ...), custom_call_target="tpu_custom_call" | custom-call | flops 822083584 | bytes 6881280 | tf_op jit(solution)/shard_map/down/pallas_call | solution.py:188
  92.7 5.5 %collective-permute-done.32 = bf16[128,1792]{1,0:T(8,128)(2,1)S(1)} collective-permute-done((bf16[128,1792]{1,0:T(8,128)(2,1)S(1)}, bf16[128,1792]{1,0:T(8,128)(2,1)S(1)}, u32[]{:S(2)}, u32[]{:S(2)}) %collective-permute-start.32) | collective-permute-done | bytes 458784 | tf_op jit(solution)/shard_map/sum3_z/ppermute | solution.py:236
  (78 shorter events, 19.3 us)
Async XLA Ops:
  0.0 15.9 %collective-permute-start.4 = (bf16[128,1792]{1,0:T(8,128)(2,1)}, bf16[128,1792]{1,0:T(8,128)(2,1)S(1)}, u32[]{:S(2)}, u32[]{:S(2)}) collective-permute-start(bf16[128,1792]{1,0:T(8,128)(2,1)} %refs_0_), channel_id=1, source_target_pairs={{0,4},{4,8},{8,12},{12,0},{1,5},{5,9},{9,13},{13,1},{2,6},{6,10},{... | collective-permute-start | bytes 1376264 | tf_op jit(solution)/shard_map/tokens1_z/ppermute | solution.py:236
  3.0 12.9 %collective-permute-start = (bf16[128,1792]{1,0:T(8,128)(2,1)}, bf16[128,1792]{1,0:T(8,128)(2,1)S(1)}, u32[]{:S(2)}, u32[]{:S(2)}) collective-permute-start(bf16[128,1792]{1,0:T(8,128)(2,1)} %refs_0_), channel_id=1, source_target_pairs={{0,2},{2,0},{1,3},{3,1},{4,6},{6,4},{5,7},{7,5},{8,10},{10,8},{9,1... | collective-permute-start | bytes 1376264 | tf_op jit(solution)/shard_map/tokens0_x/ppermute | solution.py:212
  5.2 10.7 %collective-permute-start.1 = (f32[4,128]{1,0:T(4,128)S(1)}, f32[4,128]{1,0:T(4,128)S(1)}, u32[]{:S(2)}, u32[]{:S(2)}) collective-permute-start(f32[4,128]{1,0:T(4,128)S(1)} %select_reduce_fusion), channel_id=1, source_target_pairs={{0,4},{4,8},{8,12},{12,0},{1,5},{5,9},{9,13},{13,1},{2,6},{6,10},{... | collective-permute-start | bytes 6152 | tf_op jit(solution)/shard_map/share1_z/ppermute | solution.py:236
  6.8 9.1 %collective-permute-start.2 = (f32[4,128]{1,0:T(4,128)S(1)}, f32[4,128]{1,0:T(4,128)S(1)}, u32[]{:S(2)}, u32[]{:S(2)}) collective-permute-start(f32[4,128]{1,0:T(4,128)S(1)} %select_reduce_fusion), channel_id=1, source_target_pairs={{0,8},{4,12},{8,0},{12,4},{1,9},{5,13},{9,1},{13,5},{2,10},{6,14},... | collective-permute-start | bytes 6152 | tf_op jit(solution)/shard_map/share2_z/ppermute | solution.py:236
  8.0 7.9 %collective-permute-start.3 = (f32[4,128]{1,0:T(4,128)S(1)}, f32[4,128]{1,0:T(4,128)S(1)}, u32[]{:S(2)}, u32[]{:S(2)}) collective-permute-start(f32[4,128]{1,0:T(4,128)S(1)} %select_reduce_fusion), channel_id=1, source_target_pairs={{0,12},{4,0},{8,4},{12,8},{1,13},{5,1},{9,5},{13,9},{2,14},{6,2},{... | collective-permute-start | bytes 6152 | tf_op jit(solution)/shard_map/share3_z/ppermute | solution.py:236
  16.5 13.3 %collective-permute-start.8 = (bf16[128,1792]{1,0:T(8,128)(2,1)S(1)}, bf16[128,1792]{1,0:T(8,128)(2,1)S(1)}, u32[]{:S(2)}, u32[]{:S(2)}) collective-permute-start(bf16[128,1792]{1,0:T(8,128)(2,1)S(1)} %collective-permute-done.4.refs_0_), channel_id=1, source_target_pairs={{0,2},{2,0},{1,3},{3,1},{4,6},{6,4},{5,7},{7,5},{8,10},{10,8},{9,1... | collective-permute-start | bytes 1376264 | tf_op jit(solution)/shard_map/tokens1_x/ppermute | solution.py:212
  18.0 14.0 %collective-permute-start.7 = (bf16[128,1792]{1,0:T(8,128)(2,1)S(1)}, bf16[128,1792]{1,0:T(8,128)(2,1)S(1)}, u32[]{:S(2)}, u32[]{:S(2)}) collective-permute-start(bf16[128,1792]{1,0:T(8,128)(2,1)S(1)} %collective-permute-done.4.refs_0_), channel_id=1, source_target_pairs={{0,4},{4,8},{8,12},{12,0},{1,5},{5,9},{9,13},{13,1},{2,6},{6,10},{... | collective-permute-start | bytes 1376264 | tf_op jit(solution)/shard_map/tokens2_z/ppermute | solution.py:236
  32.6 17.6 %collective-permute-start.10 = (bf16[128,1792]{1,0:T(8,128)(2,1)S(1)}, bf16[128,1792]{1,0:T(8,128)(2,1)S(1)}, u32[]{:S(2)}, u32[]{:S(2)}) collective-permute-start(bf16[128,1792]{1,0:T(8,128)(2,1)S(1)} %collective-permute-done.7.refs_0_), channel_id=1, source_target_pairs={{0,2},{2,0},{1,3},{3,1},{4,6},{6,4},{5,7},{7,5},{8,10},{10,8},{9,1... | collective-permute-start | bytes 1376264 | tf_op jit(solution)/shard_map/tokens2_x/ppermute | solution.py:212
  33.1 17.0 %collective-permute-start.9 = (bf16[128,1792]{1,0:T(8,128)(2,1)S(1)}, bf16[128,1792]{1,0:T(8,128)(2,1)S(1)}, u32[]{:S(2)}, u32[]{:S(2)}) collective-permute-start(bf16[128,1792]{1,0:T(8,128)(2,1)S(1)} %collective-permute-done.7.refs_0_), channel_id=1, source_target_pairs={{0,4},{4,8},{8,12},{12,0},{1,5},{5,9},{9,13},{13,1},{2,6},{6,10},{... | collective-permute-start | bytes 1376264 | tf_op jit(solution)/shard_map/tokens3_z/ppermute | solution.py:236
  44.5 5.6 %collective-permute-start.27 = (bf16[128,448]{1,0:T(8,128)(2,1)S(1)}, bf16[128,448]{1,0:T(8,128)(2,1)S(1)}, u32[]{:S(2)}, u32[]{:S(2)}) collective-permute-start(bf16[128,448]{1,0:T(8,128)(2,1)S(1)} %gate_up.5.refs_0_), channel_id=1, source_target_pairs={{0,2},{2,0},{1,3},{3,1},{4,6},{6,4},{5,7},{7,5},{8,10},{10,8},{9,1... | collective-permute-start | bytes 344072 | tf_op jit(solution)/shard_map/hidden1_x/ppermute | solution.py:212
  45.2 6.1 %collective-permute-start.28 = (bf16[128,448]{1,0:T(8,128)(2,1)S(1)}, bf16[128,448]{1,0:T(8,128)(2,1)S(1)}, u32[]{:S(2)}, u32[]{:S(2)}) collective-permute-start(bf16[128,448]{1,0:T(8,128)(2,1)S(1)} %gate_up.5.refs_0_), channel_id=1, source_target_pairs={{0,1},{1,0},{2,3},{3,2},{4,5},{5,4},{6,7},{7,6},{8,9},{9,8},{10,11... | collective-permute-start | bytes 344072 | tf_op jit(solution)/shard_map/hidden1_c/ppermute | solution.py:212
  50.1 3.5 %collective-permute-start.14 = (bf16[128,1792]{1,0:T(8,128)(2,1)S(1)}, bf16[128,1792]{1,0:T(8,128)(2,1)S(1)}, u32[]{:S(2)}, u32[]{:S(2)}) collective-permute-start(bf16[128,1792]{1,0:T(8,128)(2,1)S(1)} %collective-permute-done.7.refs_0_), channel_id=1, source_target_pairs={{0,1},{1,0},{2,3},{3,2},{4,5},{5,4},{6,7},{7,6},{8,9},{9,8},{10,11... | collective-permute-start | bytes 1376264 | tf_op jit(solution)/shard_map/tokens2_c/ppermute | solution.py:212
  50.7 2.9 %collective-permute-start.15 = (bf16[128,1792]{1,0:T(8,128)(2,1)S(1)}, bf16[128,1792]{1,0:T(8,128)(2,1)S(1)}, u32[]{:S(2)}, u32[]{:S(2)}) collective-permute-start(bf16[128,1792]{1,0:T(8,128)(2,1)S(1)} %collective-permute-done.10.refs_1_), channel_id=1, source_target_pairs={{0,1},{1,0},{2,3},{3,2},{4,5},{5,4},{6,7},{7,6},{8,9},{9,8},{10,11... | collective-permute-start | bytes 1376264 | tf_op jit(solution)/shard_map/tokens2_xc/ppermute | solution.py:212
  50.8 16.2 %collective-permute-start.13 = (bf16[128,1792]{1,0:T(8,128)(2,1)S(1)}, bf16[128,1792]{1,0:T(8,128)(2,1)S(1)}, u32[]{:S(2)}, u32[]{:S(2)}) collective-permute-start(bf16[128,1792]{1,0:T(8,128)(2,1)S(1)} %collective-permute-done.9.refs_0_), channel_id=1, source_target_pairs={{0,2},{2,0},{1,3},{3,1},{4,6},{6,4},{5,7},{7,5},{8,10},{10,8},{9,1... | collective-permute-start | bytes 1376264 | tf_op jit(solution)/shard_map/tokens3_x/ppermute | solution.py:212
  53.4 16.1 %collective-permute-start.30 = (bf16[128,1792]{1,0:T(8,128)(2,1)S(1)}, bf16[128,1792]{1,0:T(8,128)(2,1)S(1)}, u32[]{:S(2)}, u32[]{:S(2)}) collective-permute-start(bf16[128,1792]{1,0:T(8,128)(2,1)S(1)} %select_convert_fusion), channel_id=1, source_target_pairs={{0,4},{4,8},{8,12},{12,0},{1,5},{5,9},{9,13},{13,1},{2,6},{6,10},{... | collective-permute-start | bytes 1376264 | tf_op jit(solution)/shard_map/sum1_z/ppermute | solution.py:236
  58.0 8.5 %collective-permute-start.24 = (bf16[128,448]{1,0:T(8,128)(2,1)S(1)}, bf16[128,448]{1,0:T(8,128)(2,1)S(1)}, u32[]{:S(2)}, u32[]{:S(2)}) collective-permute-start(bf16[128,448]{1,0:T(8,128)(2,1)S(1)} %gate_up.6.refs_0_), channel_id=1, source_target_pairs={{0,2},{2,0},{1,3},{3,1},{4,6},{6,4},{5,7},{7,5},{8,10},{10,8},{9,1... | collective-permute-start | bytes 344072 | tf_op jit(solution)/shard_map/hidden2_x/ppermute | solution.py:212
  59.4 7.6 %collective-permute-start.25 = (bf16[128,448]{1,0:T(8,128)(2,1)S(1)}, bf16[128,448]{1,0:T(8,128)(2,1)S(1)}, u32[]{:S(2)}, u32[]{:S(2)}) collective-permute-start(bf16[128,448]{1,0:T(8,128)(2,1)S(1)} %gate_up.6.refs_0_), channel_id=1, source_target_pairs={{0,1},{1,0},{2,3},{3,2},{4,5},{5,4},{6,7},{7,6},{8,9},{9,8},{10,11... | collective-permute-start | bytes 344072 | tf_op jit(solution)/shard_map/hidden2_c/ppermute | solution.py:212
  66.5 3.4 %collective-permute-start.19 = (bf16[128,1792]{1,0:T(8,128)(2,1)S(1)}, bf16[128,1792]{1,0:T(8,128)(2,1)S(1)}, u32[]{:S(2)}, u32[]{:S(2)}) collective-permute-start(bf16[128,1792]{1,0:T(8,128)(2,1)S(1)} %collective-permute-done.9.refs_0_), channel_id=1, source_target_pairs={{0,1},{1,0},{2,3},{3,2},{4,5},{5,4},{6,7},{7,6},{8,9},{9,8},{10,11... | collective-permute-start | bytes 1376264 | tf_op jit(solution)/shard_map/tokens3_c/ppermute | solution.py:212
  69.8 14.4 %collective-permute-start.31 = (bf16[128,1792]{1,0:T(8,128)(2,1)S(1)}, bf16[128,1792]{1,0:T(8,128)(2,1)S(1)}, u32[]{:S(2)}, u32[]{:S(2)}) collective-permute-start(bf16[128,1792]{1,0:T(8,128)(2,1)S(1)} %add_convert_fusion.2), channel_id=1, source_target_pairs={{0,4},{4,8},{8,12},{12,0},{1,5},{5,9},{9,13},{13,1},{2,6},{6,10},{... | collective-permute-start | bytes 1376264 | tf_op jit(solution)/shard_map/sum2_z/ppermute | solution.py:236
  74.2 5.6 %collective-permute-start.21 = (bf16[128,448]{1,0:T(8,128)(2,1)S(1)}, bf16[128,448]{1,0:T(8,128)(2,1)S(1)}, u32[]{:S(2)}, u32[]{:S(2)}) collective-permute-start(bf16[128,448]{1,0:T(8,128)(2,1)S(1)} %gate_up.7.refs_0_), channel_id=1, source_target_pairs={{0,2},{2,0},{1,3},{3,1},{4,6},{6,4},{5,7},{7,5},{8,10},{10,8},{9,1... | collective-permute-start | bytes 344072 | tf_op jit(solution)/shard_map/hidden3_x/ppermute | solution.py:212
  74.8 5.0 %collective-permute-start.22 = (bf16[128,448]{1,0:T(8,128)(2,1)S(1)}, bf16[128,448]{1,0:T(8,128)(2,1)S(1)}, u32[]{:S(2)}, u32[]{:S(2)}) collective-permute-start(bf16[128,448]{1,0:T(8,128)(2,1)S(1)} %gate_up.7.refs_0_), channel_id=1, source_target_pairs={{0,1},{1,0},{2,3},{3,2},{4,5},{5,4},{6,7},{7,6},{8,9},{9,8},{10,11... | collective-permute-start | bytes 344072 | tf_op jit(solution)/shard_map/hidden3_c/ppermute | solution.py:212
  84.5 13.6 %collective-permute-start.32 = (bf16[128,1792]{1,0:T(8,128)(2,1)S(1)}, bf16[128,1792]{1,0:T(8,128)(2,1)S(1)}, u32[]{:S(2)}, u32[]{:S(2)}) collective-permute-start(bf16[128,1792]{1,0:T(8,128)(2,1)S(1)} %add_convert_fusion.1), channel_id=1, source_target_pairs={{0,4},{4,8},{8,12},{12,0},{1,5},{5,9},{9,13},{13,1},{2,6},{6,10},{... | collective-permute-start | bytes 1376264 | tf_op jit(solution)/shard_map/sum3_z/ppermute | solution.py:236
  84.6 5.0 %collective-permute-start.16 = (bf16[128,448]{1,0:T(8,128)(2,1)S(1)}, bf16[128,448]{1,0:T(8,128)(2,1)S(1)}, u32[]{:S(2)}, u32[]{:S(2)}) collective-permute-start(bf16[128,448]{1,0:T(8,128)(2,1)S(1)} %gate_up.4.refs_0_), channel_id=1, source_target_pairs={{0,2},{2,0},{1,3},{3,1},{4,6},{6,4},{5,7},{7,5},{8,10},{10,8},{9,1... | collective-permute-start | bytes 344072 | tf_op jit(solution)/shard_map/hidden0_x/ppermute | solution.py:212
  85.2 4.4 %collective-permute-start.17 = (bf16[128,448]{1,0:T(8,128)(2,1)S(1)}, bf16[128,448]{1,0:T(8,128)(2,1)S(1)}, u32[]{:S(2)}, u32[]{:S(2)}) collective-permute-start(bf16[128,448]{1,0:T(8,128)(2,1)S(1)} %gate_up.4.refs_0_), channel_id=1, source_target_pairs={{0,1},{1,0},{2,3},{3,2},{4,5},{5,4},{6,7},{7,6},{8,9},{9,8},{10,11... | collective-permute-start | bytes 344072 | tf_op jit(solution)/shard_map/hidden0_c/ppermute | solution.py:212
  (17 other events, 64.6 us)

commit v3 on v2

--- a/solution.py
+++ b/solution.py
@@ -77,43 +77,8 @@
 ROWS = (((1,), (1,)), ((), ()))
 
 
-def in_hbm(array):
-    return pltpu.with_memory_space_constraint(array, pltpu.HBM)
-
-
 def in_vmem(array):
     return pltpu.with_memory_space_constraint(array, pltpu.VMEM)
-
-
-def load_kernel(count, *refs):
-    sources, targets, sems = refs[:count], refs[-count - 1 : -1], refs[-1]
-    refs[-count - 2][...] = jnp.zeros_like(refs[-count - 2])
-    copies = [
-        pltpu.make_async_copy(source, target, sems.at[i])
-        for i, (source, target) in enumerate(zip(sources, targets))
-    ]
-    for copy in copies:
-        copy.start()
-    for copy in copies:
-        copy.wait()
-
-
-def load(arrays, *after):
-    count = len(arrays)
-    return pl.pallas_call(
-        functools.partial(load_kernel, count),
-        out_shape=[jax.ShapeDtypeStruct((8, 128), jnp.float32)]
-        + [pltpu.VMEM(a.shape, a.dtype) for a in arrays],
-        in_specs=[pl.BlockSpec(memory_space=pltpu.HBM)] * count
-        + [pl.BlockSpec(memory_space=pl.ANY)] * len(after),
-        out_specs=[pl.BlockSpec(memory_space=pltpu.VMEM)] * (count + 1),
-        scratch_shapes=[pltpu.SemaphoreType.DMA((count,))],
-        compiler_params=pltpu.CompilerParams(vmem_limit_bytes=1 * MIB),
-        cost_estimate=pl.CostEstimate(
-            flops=0, bytes_accessed=2 * sum(a.size * 2 for a in arrays), transcendentals=0
-        ),
-        name="load",
-    )(*[in_hbm(a) for a in arrays], *after)
 
 
 def gate_up_kernel(order_ref, *refs):
@@ -154,24 +119,6 @@
 
 def down_kernel(order_ref, *refs):
     pieces = refs[:4]
-    weight_ref = refs[4]
-    out_ref, blocks, sems = refs[-3:]
-    units = pieces[0].shape[1]
-    copies = []
-    for j in range(4):
-        rows = pl.ds(pl.multiple_of(order_ref[j] * units, units), units)
-        copies.append(pltpu.make_async_copy(weight_ref.at[rows, :], blocks.at[j], sems.at[j]))
-    for copy in copies:
-        copy.start()
-    total = 0.0
-    for j, piece in enumerate(pieces):
-        copies[j].wait()
-        total += jnp.dot(piece[...], blocks[j], preferred_element_type=jnp.float32)
-    out_ref[...] = total.astype(out_ref.dtype)
-
-
-def down_kernel(order_ref, *refs):
-    pieces = refs[:4]
     weight_ref, out_ref = refs[4:]
     units = pieces[0].shape[1]
     total = 0.0
@@ -243,38 +190,38 @@
             swap(beyond, "node", what + "_xc"),
         )
 
-    blocks, across, hidden = [tokens], [swap(tokens, "tensor", "tokens0_x")], []
+    gate, up, out = gate_weight[0], up_weight[0], down_weight[0]
+    shares = [dense] + [onward(dense, f"share{s}_z", s) for s in range(1, owners)]
+    blocks, across = [tokens], [swap(tokens, "tensor", "tokens0_x")]
     blocks.append(onward(tokens, "tokens1_z"))
-    shares = [dense] + [onward(dense, f"share{s}_z", s) for s in range(1, owners)]
-    gate = up = out = None
-    for s in range(1, owners):
-        known = [across[s - 1], *shares[1:]] if s == 1 else [across[s - 1], hidden[s - 2]]
-        across.append(swap(after(blocks[s], *known), "tensor", f"tokens{s}_x"))
-        if s + 1 < owners:
-            onto = after(blocks[s], *known)
-            blocks.append(onward(onto, f"tokens{s + 1}_z"))
-        k = s - 1
-        own, beyond = after(blocks[k], *known, blocks[s]), after(across[k], *known, blocks[s])
-        if s == 1:
-            gate, up, out = after(gate_weight[0]), after(up_weight[0]), after(down_weight[0])
-        hidden.append(gate_up(order, quarters(own, beyond, f"tokens{k}"), gate, up))
-        across[s] = after(across[s], hidden[k])
-    k = owners - 1
-    hidden.append(gate_up(order, quarters(blocks[k], across[k], f"tokens{k}"), gate, up))
+    hidden, terms, partial = [None] * owners, [], None
+
+    def into_hidden(s, own, beyond, *others):
+        hidden[s] = gate_up(order, quarters(own, beyond, f"tokens{s}"), gate, up, *others)
 
     def contribution(s):
-        own = after(hidden[s], across[-1]) if s == 0 else hidden[s]
+        own = hidden[s]
         beyond = swap(own, "tensor", f"hidden{s}_x")
         result = down(order, quarters(own, beyond, f"hidden{s}"), out)
         share = jnp.sum(jnp.where(mine, shares[s], 0.0), axis=0)[:, None]
         return jnp.where(share != 0, share * result.astype(jnp.float32), 0.0)
 
-    partial = None
+    known = [across[0], *shares[1:]]
     for s in range(1, owners):
+        own = after(blocks[s], *known)
+        across.append(swap(own, "tensor", f"tokens{s}_x"))
+        if s + 1 < owners:
+            blocks.append(onward(own, f"tokens{s + 1}_z"))
+        if s > 1:
+            across[s] = after(across[s], hidden[s - 1])
+        into_hidden(s, own, across[s], *terms[-1:])
         term = contribution(s)
         if partial is not None:
             term = term + partial.astype(jnp.float32)
-        partial = onward(term.astype(jnp.bfloat16), f"sum{s}_z")
+        terms.append(term.astype(jnp.bfloat16))
+        partial = onward(terms[-1], f"sum{s}_z")
+        known = [across[s]]
+    into_hidden(0, tokens, across[0], *terms[-1:])
     return (contribution(0) + partial.astype(jnp.float32)).astype(jnp.bfloat16)
 
 

time: 99.5 us -> 96.3 us (0.968)
  local copies, waits for them, and re-layouts: 12.3 us -> 5.66 us
  starting transfers between devices: 19.3 us -> 22.2 us
    unnamed x16 -> x12, local copies, waits for them, and re-layouts: 12.3 us -> 5.66 us
    ppermute x24, waiting for transfers between devices: 26.4 us -> 30.8 us  [swap(): return lax.ppermute(array, axis, SWAP)]
    ppermute x9, waiting for transfers between devices: 14.2 us -> 10.4 us  [onward(): return lax.ppermute(array, 'expert', shift)]
    ppermute x24, starting transfers between devices: 9.63 us -> 11.9 us  [swap(): return lax.ppermute(array, axis, SWAP)]
  transfers between devices with their start and end apart: 33 -> 33, of which waited for: 14 -> 12; matrix products, arithmetic and copies ran while one was open for 1% -> 2% of each run, Pallas kernels for 24% -> 25%
where the time goes in v3:
time: 96.3 us; the launch traced here: 96.1 us
  waiting for transfers between devices  41.2 us (43%)
  Pallas kernels  23.9 us (25%)
  starting transfers between devices  22.2 us (23%)
  local copies, waits for them, and re-layouts  5.66 us (6%)
  other arithmetic  2.88 us (3%)
    ppermute x24, waiting for transfers between devices, swap(): return lax.ppermute(array, axis, SWAP)  30.8 us
    pallas_call x4, Pallas kernels, gate_up(): pl.pallas_call(gate_up_kernel, out_shape=jax.ShapeDtypeStruct((rows, unit...  17.2 us
    ppermute x24, starting transfers between devices, swap(): return lax.ppermute(array, axis, SWAP)  11.9 us
    ppermute x9, waiting for transfers between devices, onward(): return lax.ppermute(array, 'expert', shift)  10.4 us
    ppermute x9, starting transfers between devices, onward(): return lax.ppermute(array, 'expert', shift)  10.3 us
    pallas_call x4, Pallas kernels, down(): pl.pallas_call(down_kernel, out_shape=jax.ShapeDtypeStruct((rows, width),...  6.66 us
    unnamed x12, local copies, waits for them, and re-layouts  5.66 us
  transfers between devices with their start and end apart: 33, of which 12 were waited for; matrix products, arithmetic and copies ran while one was open for 2% of the time, Pallas kernels for 25%

profile of v3, /device:TPU:0, one launch (start us, length us, event | category | flops | bytes accessed | tf_op | source)
XLA Modules:
  0.0 96.1 jit_solution(15053285329296200417)
XLA Ops:
  0.0 3.0 %collective-permute-start.4 = (bf16[128,1792]{1,0:T(8,128)(2,1)}, bf16[128,1792]{1,0:T(8,128)(2,1)S(1)}, u32[]{:S(2)}, u32[]{:S(2)}) collective-permute-start(bf16[128,1792]{1,0:T(8,128)(2,1)} %refs_0_.1), channel_id=1, source_target_pairs={{0,4},{4,8},{8,12},{12,0},{1,5},{5,9},{9,13},{13,1},{2,6},{6,10},{... | collective-permute-start | bytes 1376264 | tf_op jit(solution)/shard_map/tokens1_z/ppermute | solution.py:183
  3.0 1.5 %collective-permute-start = (bf16[128,1792]{1,0:T(8,128)(2,1)}, bf16[128,1792]{1,0:T(8,128)(2,1)S(1)}, u32[]{:S(2)}, u32[]{:S(2)}) collective-permute-start(bf16[128,1792]{1,0:T(8,128)(2,1)} %refs_0_.1), channel_id=1, source_target_pairs={{0,2},{2,0},{1,3},{3,1},{4,6},{6,4},{5,7},{7,5},{8,10},{10,8},{9,1... | collective-permute-start | bytes 1376264 | tf_op jit(solution)/shard_map/tokens0_x/ppermute | solution.py:159
  5.2 1.6 %collective-permute-start.5 = (f32[4,128]{1,0:T(4,128)S(1)}, f32[4,128]{1,0:T(4,128)S(1)}, u32[]{:S(2)}, u32[]{:S(2)}) collective-permute-start(f32[4,128]{1,0:T(4,128)S(1)} %select_reduce_fusion), channel_id=1, source_target_pairs={{0,4},{4,8},{8,12},{12,0},{1,5},{5,9},{9,13},{13,1},{2,6},{6,10},{... | collective-permute-start | bytes 6152 | tf_op jit(solution)/shard_map/share1_z/ppermute | solution.py:183
  8.0 2.7 %collective-permute-start.3 = (f32[4,128]{1,0:T(4,128)S(1)}, f32[4,128]{1,0:T(4,128)S(1)}, u32[]{:S(2)}, u32[]{:S(2)}) collective-permute-start(f32[4,128]{1,0:T(4,128)S(1)} %select_reduce_fusion), channel_id=1, source_target_pairs={{0,12},{4,0},{8,4},{12,8},{1,13},{5,1},{9,5},{13,9},{2,14},{6,2},{... | collective-permute-start | bytes 6152 | tf_op jit(solution)/shard_map/share3_z/ppermute | solution.py:183
  10.7 5.2 %collective-permute-done.5 = f32[4,128]{1,0:T(4,128)S(1)} collective-permute-done((f32[4,128]{1,0:T(4,128)S(1)}, f32[4,128]{1,0:T(4,128)S(1)}, u32[]{:S(2)}, u32[]{:S(2)}) %collective-permute-start.5) | collective-permute-done | bytes 2080 | tf_op jit(solution)/shard_map/share1_z/ppermute | solution.py:183
  16.0 1.6 %collective-permute-start.8 = (bf16[128,1792]{1,0:T(8,128)(2,1)S(1)}, bf16[128,1792]{1,0:T(8,128)(2,1)S(1)}, u32[]{:S(2)}, u32[]{:S(2)}) collective-permute-start(bf16[128,1792]{1,0:T(8,128)(2,1)S(1)} %collective-permute-done.4.refs_0_), channel_id=1, source_target_pairs={{0,2},{2,0},{1,3},{3,1},{4,6},{6,4},{5,7},{7,5},{8,10},{10,8},{9,1... | collective-permute-start | bytes 1376264 | tf_op jit(solution)/shard_map/tokens1_x/ppermute | solution.py:159
  18.3 9.4 %collective-permute-done.8.refs_1_ = bf16[128,1792]{1,0:T(8,128)(2,1)S(1)} collective-permute-done((bf16[128,1792]{1,0:T(8,128)(2,1)S(1)}, bf16[128,1792]{1,0:T(8,128)(2,1)S(1)}, u32[]{:S(2)}, u32[]{:S(2)}) %collective-permute-start.8) | collective-permute-done | bytes 458784 | tf_op jit(solution)/shard_map/tokens1_x/ppermute | solution.py:159
  27.7 2.7 %collective-permute-done.7.refs_0_ = bf16[128,1792]{1,0:T(8,128)(2,1)S(1)} collective-permute-done((bf16[128,1792]{1,0:T(8,128)(2,1)S(1)}, bf16[128,1792]{1,0:T(8,128)(2,1)S(1)}, u32[]{:S(2)}, u32[]{:S(2)}) %collective-permute-start.7) | collective-permute-done | bytes 458784 | tf_op jit(solution)/shard_map/tokens2_z/ppermute | solution.py:183
  31.2 2.8 %copy-done = bf16[1,448,7168]{2,1,0:T(8,128)(2,1)S(1)} copy-done((bf16[1,448,7168]{2,1,0:T(8,128)(2,1)S(1)}, bf16[1,448,7168]{2,1,0:T(8,128)(2,1)}, u32[]{:S(2)}) %copy-start) | copy-done | bytes 6422552
  34.0 2.8 %copy-done.2 = bf16[1,448,7168]{2,1,0:T(8,128)(2,1)S(1)} copy-done((bf16[1,448,7168]{2,1,0:T(8,128)(2,1)S(1)}, bf16[1,448,7168]{2,1,0:T(8,128)(2,1)}, u32[]{:S(2)}) %copy-start.2) | copy-done | bytes 6422552
  36.9 4.3 %gate_up.4.refs_0_ = bf16[128,448]{1,0:T(8,128)(2,1)S(1)} custom-call(s32[4]{0:T(128)S(1)} %pad_add_fusion.order_ref, bf16[128,1792]{1,0:T(8,128)(2,1)S(1)} %collective-permute-done.4.refs_0_, bf16[128,1792]{1,0:T(8,128)(2,1)S(1)} %collective-permute-done.8.refs_1_, bf16[128,1792]{1,0:T(8,128)(2,1)S(1)} %collective-permute-done.11.refs_2_, ...), custom_call_target="tpu_custom_call" | custom-call | flops 1644167168 | bytes 14680064 | tf_op jit(solution)/shard_map/gate_up/pallas_call | solution.py:105
  42.6 3.6 %collective-permute-done.16.refs_1_ = bf16[128,448]{1,0:T(8,128)(2,1)S(1)} collective-permute-done((bf16[128,448]{1,0:T(8,128)(2,1)S(1)}, bf16[128,448]{1,0:T(8,128)(2,1)S(1)}, u32[]{:S(2)}, u32[]{:S(2)}) %collective-permute-start.16) | collective-permute-done | bytes 114720 | tf_op jit(solution)/shard_map/hidden1_x/ppermute | solution.py:159
  48.1 1.7 %down.4 = bf16[128,1792]{1,0:T(8,128)(2,1)S(1)} custom-call(s32[4]{0:T(128)S(1)} %pad_add_fusion.order_ref, bf16[128,448]{1,0:T(8,128)(2,1)S(1)} %gate_up.4.refs_0_, bf16[128,448]{1,0:T(8,128)(2,1)S(1)} %collective-permute-done.16.refs_1_, bf16[128,448]{1,0:T(8,128)(2,1)S(1)} %collective-permute-done.17.refs_2_, ...), custom_call_target="tpu_custom_call" | custom-call | flops 822083584 | bytes 6881280 | tf_op jit(solution)/shard_map/down/pallas_call | solution.py:135
  50.3 4.3 %gate_up.5.refs_0_ = bf16[128,448]{1,0:T(8,128)(2,1)S(1)} custom-call(s32[4]{0:T(128)S(1)} %pad_add_fusion.order_ref, bf16[128,1792]{1,0:T(8,128)(2,1)S(1)} %collective-permute-done.7.refs_0_, bf16[128,1792]{1,0:T(8,128)(2,1)S(1)} %collective-permute-done.10.refs_1_, bf16[128,1792]{1,0:T(8,128)(2,1)S(1)} %collective-permute-done.14.refs_2_, ...), custom_call_target="tpu_custom_call" | custom-call | flops 1644167168 | bytes 14680064 | tf_op jit(solution)/shard_map/gate_up/pallas_call | solution.py:105
  55.5 7.0 %collective-permute-done.21.refs_1_ = bf16[128,448]{1,0:T(8,128)(2,1)S(1)} collective-permute-done((bf16[128,448]{1,0:T(8,128)(2,1)S(1)}, bf16[128,448]{1,0:T(8,128)(2,1)S(1)}, u32[]{:S(2)}, u32[]{:S(2)}) %collective-permute-start.21) | collective-permute-done | bytes 114720 | tf_op jit(solution)/shard_map/hidden2_x/ppermute | solution.py:159
  63.8 1.7 %down.5 = bf16[128,1792]{1,0:T(8,128)(2,1)S(1)} custom-call(s32[4]{0:T(128)S(1)} %pad_add_fusion.order_ref, bf16[128,448]{1,0:T(8,128)(2,1)S(1)} %gate_up.5.refs_0_, bf16[128,448]{1,0:T(8,128)(2,1)S(1)} %collective-permute-done.21.refs_1_, bf16[128,448]{1,0:T(8,128)(2,1)S(1)} %collective-permute-done.22.refs_2_, ...), custom_call_target="tpu_custom_call" | custom-call | flops 822083584 | bytes 6881280 | tf_op jit(solution)/shard_map/down/pallas_call | solution.py:135
  66.3 4.3 %gate_up.6.refs_0_ = bf16[128,448]{1,0:T(8,128)(2,1)S(1)} custom-call(s32[4]{0:T(128)S(1)} %pad_add_fusion.order_ref, bf16[128,1792]{1,0:T(8,128)(2,1)S(1)} %collective-permute-done.9.refs_0_, bf16[128,1792]{1,0:T(8,128)(2,1)S(1)} %collective-permute-done.13.refs_1_, bf16[128,1792]{1,0:T(8,128)(2,1)S(1)} %collective-permute-done.19.refs_2_, ...), custom_call_target="tpu_custom_call" | custom-call | flops 1644167168 | bytes 14680064 | tf_op jit(solution)/shard_map/gate_up/pallas_call | solution.py:105
  70.6 1.3 %collective-permute-start.25 = (bf16[128,448]{1,0:T(8,128)(2,1)S(1)}, bf16[128,448]{1,0:T(8,128)(2,1)S(1)}, u32[]{:S(2)}, u32[]{:S(2)}) collective-permute-start(bf16[128,448]{1,0:T(8,128)(2,1)S(1)} %gate_up.6.refs_0_), channel_id=1, source_target_pairs={{0,2},{2,0},{1,3},{3,1},{4,6},{6,4},{5,7},{7,5},{8,10},{10,8},{9,1... | collective-permute-start | bytes 344072 | tf_op jit(solution)/shard_map/hidden3_x/ppermute | solution.py:159
  72.5 3.6 %collective-permute-done.25.refs_1_ = bf16[128,448]{1,0:T(8,128)(2,1)S(1)} collective-permute-done((bf16[128,448]{1,0:T(8,128)(2,1)S(1)}, bf16[128,448]{1,0:T(8,128)(2,1)S(1)}, u32[]{:S(2)}, u32[]{:S(2)}) %collective-permute-start.25) | collective-permute-done | bytes 114720 | tf_op jit(solution)/shard_map/hidden3_x/ppermute | solution.py:159
  77.4 1.7 %down.6 = bf16[128,1792]{1,0:T(8,128)(2,1)S(1)} custom-call(s32[4]{0:T(128)S(1)} %pad_add_fusion.order_ref, bf16[128,448]{1,0:T(8,128)(2,1)S(1)} %gate_up.6.refs_0_, bf16[128,448]{1,0:T(8,128)(2,1)S(1)} %collective-permute-done.25.refs_1_, bf16[128,448]{1,0:T(8,128)(2,1)S(1)} %collective-permute-done.26.refs_2_, ...), custom_call_target="tpu_custom_call" | custom-call | flops 822083584 | bytes 6881280 | tf_op jit(solution)/shard_map/down/pallas_call | solution.py:135
  79.1 1.6 %collective-permute-done.28 = bf16[128,1792]{1,0:T(8,128)(2,1)S(1)} collective-permute-done((bf16[128,1792]{1,0:T(8,128)(2,1)S(1)}, bf16[128,1792]{1,0:T(8,128)(2,1)S(1)}, u32[]{:S(2)}, u32[]{:S(2)}) %collective-permute-start.28) | collective-permute-done | bytes 458784 | tf_op jit(solution)/shard_map/sum2_z/ppermute | solution.py:183
  81.4 4.3 %gate_up.7.refs_0_ = bf16[128,448]{1,0:T(8,128)(2,1)S(1)} custom-call(s32[4]{0:T(128)S(1)} %pad_add_fusion.order_ref, bf16[128,1792]{1,0:T(8,128)(2,1)S(1)} %copy-done.5, bf16[128,1792]{1,0:T(8,128)(2,1)S(1)} %collective-permute-done.refs_1_, bf16[128,1792]{1,0:T(8,128)(2,1)S(1)} %collective-permute-done.1.refs_2_, ...), custom_call_target="tpu_custom_call" | custom-call | flops 1644167168 | bytes 14680064 | tf_op jit(solution)/shard_map/gate_up/pallas_call | solution.py:105
  86.8 4.3 %collective-permute-done.29.refs_1_ = bf16[128,448]{1,0:T(8,128)(2,1)S(1)} collective-permute-done((bf16[128,448]{1,0:T(8,128)(2,1)S(1)}, bf16[128,448]{1,0:T(8,128)(2,1)S(1)}, u32[]{:S(2)}, u32[]{:S(2)}) %collective-permute-start.29) | collective-permute-done | bytes 114720 | tf_op jit(solution)/shard_map/hidden0_x/ppermute | solution.py:159
  92.4 1.7 %down.7 = bf16[128,1792]{1,0:T(8,128)(2,1)S(1)} custom-call(s32[4]{0:T(128)S(1)} %pad_add_fusion.order_ref, bf16[128,448]{1,0:T(8,128)(2,1)S(1)} %gate_up.7.refs_0_, bf16[128,448]{1,0:T(8,128)(2,1)S(1)} %collective-permute-done.29.refs_1_, bf16[128,448]{1,0:T(8,128)(2,1)S(1)} %collective-permute-done.30.refs_2_, ...), custom_call_target="tpu_custom_call" | custom-call | flops 822083584 | bytes 6881280 | tf_op jit(solution)/shard_map/down/pallas_call | solution.py:135
  (74 shorter events, 17.3 us)
Async XLA Ops:
  0.0 15.9 %collective-permute-start.4 = (bf16[128,1792]{1,0:T(8,128)(2,1)}, bf16[128,1792]{1,0:T(8,128)(2,1)S(1)}, u32[]{:S(2)}, u32[]{:S(2)}) collective-permute-start(bf16[128,1792]{1,0:T(8,128)(2,1)} %refs_0_.1), channel_id=1, source_target_pairs={{0,4},{4,8},{8,12},{12,0},{1,5},{5,9},{9,13},{13,1},{2,6},{6,10},{... | collective-permute-start | bytes 1376264 | tf_op jit(solution)/shard_map/tokens1_z/ppermute | solution.py:183
  3.0 12.9 %collective-permute-start = (bf16[128,1792]{1,0:T(8,128)(2,1)}, bf16[128,1792]{1,0:T(8,128)(2,1)S(1)}, u32[]{:S(2)}, u32[]{:S(2)}) collective-permute-start(bf16[128,1792]{1,0:T(8,128)(2,1)} %refs_0_.1), channel_id=1, source_target_pairs={{0,2},{2,0},{1,3},{3,1},{4,6},{6,4},{5,7},{7,5},{8,10},{10,8},{9,1... | collective-permute-start | bytes 1376264 | tf_op jit(solution)/shard_map/tokens0_x/ppermute | solution.py:159
  5.2 10.7 %collective-permute-start.5 = (f32[4,128]{1,0:T(4,128)S(1)}, f32[4,128]{1,0:T(4,128)S(1)}, u32[]{:S(2)}, u32[]{:S(2)}) collective-permute-start(f32[4,128]{1,0:T(4,128)S(1)} %select_reduce_fusion), channel_id=1, source_target_pairs={{0,4},{4,8},{8,12},{12,0},{1,5},{5,9},{9,13},{13,1},{2,6},{6,10},{... | collective-permute-start | bytes 6152 | tf_op jit(solution)/shard_map/share1_z/ppermute | solution.py:183
  6.8 9.1 %collective-permute-start.6 = (f32[4,128]{1,0:T(4,128)S(1)}, f32[4,128]{1,0:T(4,128)S(1)}, u32[]{:S(2)}, u32[]{:S(2)}) collective-permute-start(f32[4,128]{1,0:T(4,128)S(1)} %select_reduce_fusion), channel_id=1, source_target_pairs={{0,8},{4,12},{8,0},{12,4},{1,9},{5,13},{9,1},{13,5},{2,10},{6,14},... | collective-permute-start | bytes 6152 | tf_op jit(solution)/shard_map/share2_z/ppermute | solution.py:183
  8.0 7.9 %collective-permute-start.3 = (f32[4,128]{1,0:T(4,128)S(1)}, f32[4,128]{1,0:T(4,128)S(1)}, u32[]{:S(2)}, u32[]{:S(2)}) collective-permute-start(f32[4,128]{1,0:T(4,128)S(1)} %select_reduce_fusion), channel_id=1, source_target_pairs={{0,12},{4,0},{8,4},{12,8},{1,13},{5,1},{9,5},{13,9},{2,14},{6,2},{... | collective-permute-start | bytes 6152 | tf_op jit(solution)/shard_map/share3_z/ppermute | solution.py:183
  16.0 11.7 %collective-permute-start.8 = (bf16[128,1792]{1,0:T(8,128)(2,1)S(1)}, bf16[128,1792]{1,0:T(8,128)(2,1)S(1)}, u32[]{:S(2)}, u32[]{:S(2)}) collective-permute-start(bf16[128,1792]{1,0:T(8,128)(2,1)S(1)} %collective-permute-done.4.refs_0_), channel_id=1, source_target_pairs={{0,2},{2,0},{1,3},{3,1},{4,6},{6,4},{5,7},{7,5},{8,10},{10,8},{9,1... | collective-permute-start | bytes 1376264 | tf_op jit(solution)/shard_map/tokens1_x/ppermute | solution.py:159
  17.5 12.9 %collective-permute-start.7 = (bf16[128,1792]{1,0:T(8,128)(2,1)S(1)}, bf16[128,1792]{1,0:T(8,128)(2,1)S(1)}, u32[]{:S(2)}, u32[]{:S(2)}) collective-permute-start(bf16[128,1792]{1,0:T(8,128)(2,1)S(1)} %collective-permute-done.4.refs_0_), channel_id=1, source_target_pairs={{0,4},{4,8},{8,12},{12,0},{1,5},{5,9},{9,13},{13,1},{2,6},{6,10},{... | collective-permute-start | bytes 1376264 | tf_op jit(solution)/shard_map/tokens2_z/ppermute | solution.py:183
  18.3 12.9 %collective-permute-start.11 = (bf16[128,1792]{1,0:T(8,128)(2,1)S(1)}, bf16[128,1792]{1,0:T(8,128)(2,1)S(1)}, u32[]{:S(2)}, u32[]{:S(2)}) collective-permute-start(bf16[128,1792]{1,0:T(8,128)(2,1)S(1)} %collective-permute-done.4.refs_0_), channel_id=1, source_target_pairs={{0,1},{1,0},{2,3},{3,2},{4,5},{5,4},{6,7},{7,6},{8,9},{9,8},{10,11... | collective-permute-start | bytes 1376264 | tf_op jit(solution)/shard_map/tokens1_c/ppermute | solution.py:159
  30.4 16.3 %collective-permute-start.10 = (bf16[128,1792]{1,0:T(8,128)(2,1)S(1)}, bf16[128,1792]{1,0:T(8,128)(2,1)S(1)}, u32[]{:S(2)}, u32[]{:S(2)}) collective-permute-start(bf16[128,1792]{1,0:T(8,128)(2,1)S(1)} %collective-permute-done.7.refs_0_), channel_id=1, source_target_pairs={{0,2},{2,0},{1,3},{3,1},{4,6},{6,4},{5,7},{7,5},{8,10},{10,8},{9,1... | collective-permute-start | bytes 1376264 | tf_op jit(solution)/shard_map/tokens2_x/ppermute | solution.py:159
  31.2 15.6 %collective-permute-start.9 = (bf16[128,1792]{1,0:T(8,128)(2,1)S(1)}, bf16[128,1792]{1,0:T(8,128)(2,1)S(1)}, u32[]{:S(2)}, u32[]{:S(2)}) collective-permute-start(bf16[128,1792]{1,0:T(8,128)(2,1)S(1)} %collective-permute-done.7.refs_0_), channel_id=1, source_target_pairs={{0,4},{4,8},{8,12},{12,0},{1,5},{5,9},{9,13},{13,1},{2,6},{6,10},{... | collective-permute-start | bytes 1376264 | tf_op jit(solution)/shard_map/tokens3_z/ppermute | solution.py:183
  41.2 5.0 %collective-permute-start.16 = (bf16[128,448]{1,0:T(8,128)(2,1)S(1)}, bf16[128,448]{1,0:T(8,128)(2,1)S(1)}, u32[]{:S(2)}, u32[]{:S(2)}) collective-permute-start(bf16[128,448]{1,0:T(8,128)(2,1)S(1)} %gate_up.4.refs_0_), channel_id=1, source_target_pairs={{0,2},{2,0},{1,3},{3,1},{4,6},{6,4},{5,7},{7,5},{8,10},{10,8},{9,1... | collective-permute-start | bytes 344072 | tf_op jit(solution)/shard_map/hidden1_x/ppermute | solution.py:159
  42.6 5.5 %collective-permute-start.17 = (bf16[128,448]{1,0:T(8,128)(2,1)S(1)}, bf16[128,448]{1,0:T(8,128)(2,1)S(1)}, u32[]{:S(2)}, u32[]{:S(2)}) collective-permute-start(bf16[128,448]{1,0:T(8,128)(2,1)S(1)} %gate_up.4.refs_0_), channel_id=1, source_target_pairs={{0,1},{1,0},{2,3},{3,2},{4,5},{5,4},{6,7},{7,6},{8,9},{9,8},{10,11... | collective-permute-start | bytes 344072 | tf_op jit(solution)/shard_map/hidden1_c/ppermute | solution.py:159
  46.8 16.2 %collective-permute-start.13 = (bf16[128,1792]{1,0:T(8,128)(2,1)S(1)}, bf16[128,1792]{1,0:T(8,128)(2,1)S(1)}, u32[]{:S(2)}, u32[]{:S(2)}) collective-permute-start(bf16[128,1792]{1,0:T(8,128)(2,1)S(1)} %collective-permute-done.9.refs_0_), channel_id=1, source_target_pairs={{0,2},{2,0},{1,3},{3,1},{4,6},{6,4},{5,7},{7,5},{8,10},{10,8},{9,1... | collective-permute-start | bytes 1376264 | tf_op jit(solution)/shard_map/tokens3_x/ppermute | solution.py:159
  50.0 15.5 %collective-permute-start.24 = (bf16[128,1792]{1,0:T(8,128)(2,1)S(1)}, bf16[128,1792]{1,0:T(8,128)(2,1)S(1)}, u32[]{:S(2)}, u32[]{:S(2)}) collective-permute-start(bf16[128,1792]{1,0:T(8,128)(2,1)S(1)} %select_convert_fusion.refs_6_), channel_id=1, source_target_pairs={{0,4},{4,8},{8,12},{12,0},{1,5},{5,9},{9,13},{13,1},{2,6},{6,10},{... | collective-permute-start | bytes 1376264 | tf_op jit(solution)/shard_map/sum1_z/ppermute | solution.py:183
  54.6 7.9 %collective-permute-start.21 = (bf16[128,448]{1,0:T(8,128)(2,1)S(1)}, bf16[128,448]{1,0:T(8,128)(2,1)S(1)}, u32[]{:S(2)}, u32[]{:S(2)}) collective-permute-start(bf16[128,448]{1,0:T(8,128)(2,1)S(1)} %gate_up.5.refs_0_), channel_id=1, source_target_pairs={{0,2},{2,0},{1,3},{3,1},{4,6},{6,4},{5,7},{7,5},{8,10},{10,8},{9,1... | collective-permute-start | bytes 344072 | tf_op jit(solution)/shard_map/hidden2_x/ppermute | solution.py:159
  55.5 7.6 %collective-permute-start.22 = (bf16[128,448]{1,0:T(8,128)(2,1)S(1)}, bf16[128,448]{1,0:T(8,128)(2,1)S(1)}, u32[]{:S(2)}, u32[]{:S(2)}) collective-permute-start(bf16[128,448]{1,0:T(8,128)(2,1)S(1)} %gate_up.5.refs_0_), channel_id=1, source_target_pairs={{0,1},{1,0},{2,3},{3,2},{4,5},{5,4},{6,7},{7,6},{8,9},{9,8},{10,11... | collective-permute-start | bytes 344072 | tf_op jit(solution)/shard_map/hidden2_c/ppermute | solution.py:159
  65.9 14.9 %collective-permute-start.28 = (bf16[128,1792]{1,0:T(8,128)(2,1)S(1)}, bf16[128,1792]{1,0:T(8,128)(2,1)S(1)}, u32[]{:S(2)}, u32[]{:S(2)}) collective-permute-start(bf16[128,1792]{1,0:T(8,128)(2,1)S(1)} %add_convert_fusion.2.refs_6_), channel_id=1, source_target_pairs={{0,4},{4,8},{8,12},{12,0},{1,5},{5,9},{9,13},{13,1},{2,6},{6,10},{... | collective-permute-start | bytes 1376264 | tf_op jit(solution)/shard_map/sum2_z/ppermute | solution.py:183
  70.6 5.4 %collective-permute-start.25 = (bf16[128,448]{1,0:T(8,128)(2,1)S(1)}, bf16[128,448]{1,0:T(8,128)(2,1)S(1)}, u32[]{:S(2)}, u32[]{:S(2)}) collective-permute-start(bf16[128,448]{1,0:T(8,128)(2,1)S(1)} %gate_up.6.refs_0_), channel_id=1, source_target_pairs={{0,2},{2,0},{1,3},{3,1},{4,6},{6,4},{5,7},{7,5},{8,10},{10,8},{9,1... | collective-permute-start | bytes 344072 | tf_op jit(solution)/shard_map/hidden3_x/ppermute | solution.py:159
  72.0 9.4 %collective-permute-start.1 = (bf16[128,1792]{1,0:T(8,128)(2,1)S(1)}, bf16[128,1792]{1,0:T(8,128)(2,1)S(1)}, u32[]{:S(2)}, u32[]{:S(2)}) collective-permute-start(bf16[128,1792]{1,0:T(8,128)(2,1)S(1)} %copy-done.5), channel_id=1, source_target_pairs={{0,1},{1,0},{2,3},{3,2},{4,5},{5,4},{6,7},{7,6},{8,9},{9,8},{10,11... | collective-permute-start | bytes 1376264 | tf_op jit(solution)/shard_map/tokens0_c/ppermute | solution.py:159
  72.0 4.6 %collective-permute-start.26 = (bf16[128,448]{1,0:T(8,128)(2,1)S(1)}, bf16[128,448]{1,0:T(8,128)(2,1)S(1)}, u32[]{:S(2)}, u32[]{:S(2)}) collective-permute-start(bf16[128,448]{1,0:T(8,128)(2,1)S(1)} %gate_up.6.refs_0_), channel_id=1, source_target_pairs={{0,1},{1,0},{2,3},{3,2},{4,5},{5,4},{6,7},{7,6},{8,9},{9,8},{10,11... | collective-permute-start | bytes 344072 | tf_op jit(solution)/shard_map/hidden3_c/ppermute | solution.py:159
  76.1 5.3 %collective-permute-start.2 = (bf16[128,1792]{1,0:T(8,128)(2,1)S(1)}, bf16[128,1792]{1,0:T(8,128)(2,1)S(1)}, u32[]{:S(2)}, u32[]{:S(2)}) collective-permute-start(bf16[128,1792]{1,0:T(8,128)(2,1)S(1)} %collective-permute-done.refs_1_), channel_id=1, source_target_pairs={{0,1},{1,0},{2,3},{3,2},{4,5},{5,4},{6,7},{7,6},{8,9},{9,8},{10,11... | collective-permute-start | bytes 1376264 | tf_op jit(solution)/shard_map/tokens0_xc/ppermute | solution.py:159
  81.1 13.9 %collective-permute-start.32 = (bf16[128,1792]{1,0:T(8,128)(2,1)S(1)}, bf16[128,1792]{1,0:T(8,128)(2,1)S(1)}, u32[]{:S(2)}, u32[]{:S(2)}) collective-permute-start(bf16[128,1792]{1,0:T(8,128)(2,1)S(1)} %add_convert_fusion.1.refs_6_), channel_id=1, source_target_pairs={{0,4},{4,8},{8,12},{12,0},{1,5},{5,9},{9,13},{13,1},{2,6},{6,10},{... | collective-permute-start | bytes 1376264 | tf_op jit(solution)/shard_map/sum3_z/ppermute | solution.py:183
  85.7 5.4 %collective-permute-start.29 = (bf16[128,448]{1,0:T(8,128)(2,1)S(1)}, bf16[128,448]{1,0:T(8,128)(2,1)S(1)}, u32[]{:S(2)}, u32[]{:S(2)}) collective-permute-start(bf16[128,448]{1,0:T(8,128)(2,1)S(1)} %gate_up.7.refs_0_), channel_id=1, source_target_pairs={{0,2},{2,0},{1,3},{3,1},{4,6},{6,4},{5,7},{7,5},{8,10},{10,8},{9,1... | collective-permute-start | bytes 344072 | tf_op jit(solution)/shard_map/hidden0_x/ppermute | solution.py:159
  86.8 4.3 %collective-permute-start.30 = (bf16[128,448]{1,0:T(8,128)(2,1)S(1)}, bf16[128,448]{1,0:T(8,128)(2,1)S(1)}, u32[]{:S(2)}, u32[]{:S(2)}) collective-permute-start(bf16[128,448]{1,0:T(8,128)(2,1)S(1)} %gate_up.7.refs_0_), channel_id=1, source_target_pairs={{0,1},{1,0},{2,3},{3,2},{4,5},{5,4},{6,7},{7,6},{8,9},{9,8},{10,11... | collective-permute-start | bytes 344072 | tf_op jit(solution)/shard_map/hidden0_c/ppermute | solution.py:159
  (15 other events, 69.7 us)
